TPU v7x, 512 devices: a whole 4x4x16 slice. The times are simulated.
512 devices in a mesh: section: 16 (over z), kv: 8 (over x, core), tp: 4 (over y).
Axes of the slice: x: 4, y: 4, z: 16, core: 2. Of those that a mesh axis runs over, the one named last changes fastest.
Arguments:
- arriving: bfloat16 [16, 128, 4096], P('section', None, ('kv', 'tp')), may hold values from -24 to 24
- entering: bfloat16 [1, 128, 4096], P(None, None, ('kv', 'tp')), may hold values from -6 to 6
- gain_attention: float32 [16, 4096], P('section'), may hold values from 0.1 to 1.9
- gain_key: float32 [16, 4096], P('section'), may hold values from -2 to 2
- decay_rate: float32 [16, 32], P('section', ('kv', 'tp')), may hold values from 0.001953125 to 0.06
- state_in: float32 [16, 32, 128, 128], P('section', ('kv', 'tp')), may hold values from -4 to 4
- gain_linear: float32 [16, 4096], P('section', ('kv', 'tp')), may hold values from 0.1 to 1.9
- gain_feed: float32 [16, 4096], P('section'), may hold values from 0.1 to 1.9
- gate_up: bfloat16 [16, 4608, 2, 4096], P('section', ('kv', 'tp')), may hold values from -0.09375 to 0.09375
- down_weight: bfloat16 [16, 4608, 4096], P('section', ('kv', 'tp')), may hold values from -0.15625 to 0.15625
- prefix_keys: bfloat16 [16, 512, 8, 512], P('section', 'kv', None, 'tp'), may hold values from -1500 to 1500
- prefix_values: bfloat16 [16, 512, 8, 512], P('section', 'kv', None, 'tp'), may hold values from -6 to 6
- lengths: int32 [16, 8], P('section'), may hold values from 1 to 64, 288 in all within a row
Outputs:
- arrived: bfloat16 [2, 16, 128, 4096], P(None, 'section', None, ('kv', 'tp'))
- state_out: float32 [16, 32, 128, 128], P('section', ('kv', 'tp'))
Inputs may be any that keep to these rules, and one draw needn't show every extreme that they name: `lengths`: in every section one shard is full (64 rows).
All inputs are finite; a program needn't handle non-finite values.
Results may differ from a plain program's by a relative error of at most 0.025.
Values may be sent and summed in bfloat16 or wider, within the bound.
No kernel may reach another device: no remote copies, remote signals or barrier semaphores. Data moves between devices by JAX's collectives and lax.ppermute only.
A program may use at most 64 MiB of HBM per device.

v0:
```python
import jax
import jax.numpy as jnp
from jax import lax
from jax.sharding import PartitionSpec as P

TICKS = 2


def joined(value, axis, join):
    pieces = jax.tree.map(lambda part: lax.all_gather(part, axis), value)
    head = jax.tree.map(lambda part: part[0], pieces)
    tail = jax.tree.map(lambda part: part[1:], pieces)
    so_far, _ = lax.scan(lambda so_far, slab: (join(so_far, slab), None), head, tail)
    return so_far


def passed_along(shard, axis, by):
    size = lax.axis_size(axis)
    return lax.ppermute(shard, axis, [(i, (i + by) % size) for i in range(size)])


def rms_scale(values):
    return lax.rsqrt(jnp.mean(values * values, axis=-1, keepdims=True) + 1e-06)


def lightning(head_queries, head_keys, head_values, decays, memory):
    tokens = head_queries.shape[0]
    head_size = head_queries.shape[2]
    positions = jnp.arange(tokens).astype(jnp.float32)
    distance = positions[:, None] - positions[None, :]
    causal = distance >= 0.0
    decay_mask = jnp.exp(-decays[:, None, None] * jnp.where(causal, distance, 0.0)[None])
    decay_mask = jnp.where(causal[None], decay_mask, 0.0)
    scores = jnp.einsum("thc,shc->hts", head_queries, head_keys, preferred_element_type=jnp.float32)
    weights = (scores * decay_mask * head_size ** (-0.5)).astype(jnp.bfloat16)
    within = jnp.einsum("hts,shc->thc", weights, head_values, preferred_element_type=jnp.float32)
    carry_scale = jnp.exp(-decays[None, :] * (positions[:, None] + 1.0))
    carried = (
        jnp.einsum(
            "thc,hce->the",
            head_queries.astype(jnp.float32),
            memory,
            precision=lax.Precision.HIGHEST,
        )
        * carry_scale[:, :, None]
    )
    tail_scale = jnp.exp(-decays[None, :] * (tokens - 1.0 - positions[:, None]))
    update = jnp.einsum(
        "shc,she->hce",
        head_keys.astype(jnp.float32) * tail_scale[:, :, None],
        head_values.astype(jnp.float32),
        precision=lax.Precision.HIGHEST,
    )
    new_memory = memory * jnp.exp(-decays * tokens)[:, None, None] + update * head_size ** (-0.5)
    return (within + carried, new_memory)


def attend(head_queries, all_keys, all_values, allowed):
    head_size = head_queries.shape[2]
    scores = jnp.einsum("thc,khc->htk", head_queries, all_keys, preferred_element_type=jnp.float32)
    scores = jnp.where(allowed[None], scores * head_size ** (-0.5), -1e30)
    row_max = jnp.max(scores, axis=-1)
    probabilities = jnp.where(allowed[None], jnp.exp(scores - row_max[..., None]), 0.0)
    row_sum = jnp.sum(probabilities, axis=-1)
    weighted = jnp.einsum(
        "htk,khc->htc",
        probabilities.astype(jnp.bfloat16),
        all_values,
        preferred_element_type=jnp.float32,
    )
    return (row_max, row_sum, weighted)


def join_partials(first, second):
    highest = jnp.maximum(first[0], second[0])
    first_scale = jnp.exp(first[0] - highest)
    second_scale = jnp.exp(second[0] - highest)
    return (
        highest,
        first[1] * first_scale + second[1] * second_scale,
        first[2] * first_scale[..., None] + second[2] * second_scale[..., None],
    )


def per_device(
    arriving,
    entering,
    gain_attention,
    gain_key,
    decay_rate,
    state_in,
    gain_linear,
    gain_feed,
    gate_up,
    down_weight,
    prefix_keys,
    prefix_values,
    lengths,
):
    kv_count = lax.axis_size("kv")
    tp_count = lax.axis_size("tp")
    kv_place = lax.axis_index("kv")
    tp_place = lax.axis_index("tp")
    block_place = lax.axis_index(("kv", "tp"))
    section_place = lax.axis_index("section")
    incoming = arriving[0]
    tokens = incoming.shape[0]
    block_width = incoming.shape[1]
    local_heads = state_in.shape[1]
    head_size = state_in.shape[3]
    attention_gain = gain_attention[0]
    key_gain = gain_key[0]
    decays = decay_rate[0]
    memory = state_in[0]
    linear_gain = gain_linear[0].reshape(local_heads, head_size)
    feed_gain = gain_feed[0]
    weights_in = gate_up[0]
    weights_out = down_weight[0]
    shard_rows = prefix_keys.shape[1]
    keys_before = prefix_keys[0]
    values_before = prefix_values[0]
    valid_count = lax.dynamic_index_in_dim(lengths[0], kv_place, 0, keepdims=False)
    prefix_mask = jnp.broadcast_to(
        (jnp.arange(shard_rows) < valid_count)[None], (tokens, shard_rows)
    )
    offset = block_place * block_width
    past_keys = []
    past_values = []
    arrived = []
    for tick_index in range(TICKS):
        assembled = lax.all_gather(incoming, ("kv", "tp"), axis=1, tiled=True)
        widened = assembled.astype(jnp.float32)
        normed = widened * rms_scale(widened) * attention_gain
        queries = normed.astype(jnp.bfloat16)
        key_rows = (normed * key_gain).astype(jnp.bfloat16)
        own_queries = lax.dynamic_slice_in_dim(queries, offset, block_width, 1).reshape(
            tokens, local_heads, head_size
        )
        own_keys = lax.dynamic_slice_in_dim(key_rows, offset, block_width, 1).reshape(
            tokens, local_heads, head_size
        )
        tp_queries = lax.dynamic_index_in_dim(
            queries.reshape(tokens, kv_count, tp_count, local_heads * head_size),
            tp_place,
            2,
            keepdims=False,
        )
        tp_keys = lax.dynamic_index_in_dim(
            key_rows.reshape(tokens, kv_count, tp_count, local_heads * head_size),
            tp_place,
            2,
            keepdims=False,
        )
        lin_raw, memory = lightning(own_queries, own_keys, own_queries, decays, memory)
        linear = lin_raw * rms_scale(lin_raw) * linear_gain
        past_keys.append(tp_keys)
        past_values.append(tp_queries)
        window_keys = jnp.concatenate(past_keys, axis=0)
        window_values = jnp.concatenate(past_values, axis=0)
        row_place = tick_index * tokens + jnp.arange(tokens)

        def with_own():
            own_place = jnp.arange(window_keys.shape[0])
            allowed = jnp.concatenate(
                [prefix_mask, own_place[None, :] <= row_place[:, None]], axis=1
            )
            return attend(
                tp_queries,
                jnp.concatenate([keys_before, window_keys], axis=0),
                jnp.concatenate([values_before, window_values], axis=0),
                allowed,
            )

        def without_own():
            return attend(tp_queries, keys_before, values_before, prefix_mask)

        row_max, row_sum, weighted = lax.cond(kv_place == 0, with_own, without_own)
        row_max, row_sum, weighted = joined((row_max, row_sum, weighted), "kv", join_partials)
        head_start = kv_place * local_heads
        row_sum = lax.dynamic_slice_in_dim(row_sum, head_start, local_heads, 0)
        weighted = lax.dynamic_slice_in_dim(weighted, head_start, local_heads, 0)
        softmax_out = jnp.transpose(weighted / row_sum[..., None], (1, 0, 2))
        mixed_block = (
            incoming.astype(jnp.float32) + (linear + softmax_out).reshape(tokens, block_width)
        ).astype(jnp.bfloat16)
        mixed_in = lax.all_gather(mixed_block, ("kv", "tp"), axis=1, tiled=True)
        mixed_wide = mixed_in.astype(jnp.float32)
        feed_in = (mixed_wide * rms_scale(mixed_wide) * feed_gain).astype(jnp.bfloat16)
        gate_cols = lax.dot_general(
            weights_in[:, 0, :],
            feed_in,
            (((1,), (1,)), ((), ())),
            preferred_element_type=jnp.float32,
        )
        up_cols = lax.dot_general(
            weights_in[:, 1, :],
            feed_in,
            (((1,), (1,)), ((), ())),
            preferred_element_type=jnp.float32,
        )
        hidden_cols = (jax.nn.silu(gate_cols) * up_cols).astype(jnp.bfloat16)
        down_part = lax.psum_scatter(
            lax.dot_general(
                weights_out,
                hidden_cols,
                (((0,), (0,)), ((), ())),
                preferred_element_type=jnp.float32,
            ).astype(jnp.bfloat16),
            ("kv", "tp"),
            scatter_dimension=0,
            tiled=True,
        ).astype(jnp.float32)
        finished = (mixed_block.astype(jnp.float32) + jnp.transpose(down_part)).astype(jnp.bfloat16)
        passed = passed_along(finished, "section", 1)
        arrived.append(passed)
        if tick_index + 1 < TICKS:
            incoming = jnp.where(section_place == 0, entering[tick_index], passed)
    return (jnp.stack(arrived)[:, None], memory[None])


def solution(mesh):
    in_specs = (
        P("section", None, ("kv", "tp")),
        P(None, None, ("kv", "tp")),
        P("section", None),
        P("section", None),
        P("section", ("kv", "tp")),
        P("section", ("kv", "tp"), None, None),
        P("section", ("kv", "tp")),
        P("section", None),
        P("section", ("kv", "tp"), None, None),
        P("section", ("kv", "tp"), None),
        P("section", "kv", None, "tp"),
        P("section", "kv", None, "tp"),
        P("section", None),
    )
    out_specs = (P(None, "section", None, ("kv", "tp")), P("section", ("kv", "tp"), None, None))
    return jax.shard_map(
        per_device, mesh=mesh, in_specs=in_specs, out_specs=out_specs, check_vma=False
    )
```

profile of v0, /device:TPU:1, one launch (start us, length us, event | category | flops | bytes accessed | tf_op | source)
XLA Modules:
  0.0 625.9 jit_solution(16015072934949090644)
XLA Ops:
  12.5 63.1 %all-gather.20.cloned.1.call-done = bf16[1,128,4096]{1,2,0:T(8,128)(2,1)} async-done(((bf16[1,128,128]{1,2,0:T(8,128)(2,1)}), bf16[1,128,4096]{1,2,0:T(8,128)(2,1)}) %all-gather.20.cloned.1.call-update) | async-done | bytes 1048592 | tf_op jit(solution)/shard_map/all_gather | solution.py:131
  77.4 3.3 fusion.81
  83.5 3.7 conditional.2
  88.9 13.5 %all-gather.1 = f32[64,128]{1,0:T(8,128)S(1)} all-gather(f32[8,128]{1,0:T(8,128)} %get-tuple-element.180), channel_id=3, replica_groups=mesh['section'=16,'kv'=8,'tp'=4] {'kv'}, dimensions={0}, use_global_device_ids=true | all-gather | bytes 36864 | tf_op jit(solution)/shard_map/all_gather | solution.py:10
  102.3 12.8 %all-gather.2 = f32[64,128]{1,0:T(8,128)S(1)} all-gather(f32[8,128]{1,0:T(8,128)S(1)} %get-tuple-element.181), channel_id=4, replica_groups=mesh['section'=16,'kv'=8,'tp'=4] {'kv'}, dimensions={0}, use_global_device_ids=true | all-gather | bytes 36864 | tf_op jit(solution)/shard_map/all_gather | solution.py:10
  116.6 11.0 %all-gather.22.cloned.1.call-done = f32[64,128,128]{2,1,0:T(8,128)} async-done(((f32[8,128,128]{2,1,0:T(8,128)}), f32[64,128,128]{2,1,0:T(8,128)}) %all-gather.22.cloned.1.call-update) | async-done | bytes 4194320 | tf_op jit(solution)/shard_map/all_gather | solution.py:10
  127.5 4.3 slice.75
  131.9 10.9 %while.28 = (s32[]{:T(128)}, f32[8,128]{1,0:T(8,128)S(1)}, f32[8,128]{1,0:T(8,128)S(1)}, f32[8,128,128]{2,1,0:T(8,128)S(1)}, f32[7,8,128]{2,1,0:T(8,128)S(1)}, /...) while((s32[]{:T(128)}, f32[8,128]{1,0:T(8,128)S(1)}, f32[8,128]{1,0:T(8,128)S(1)}, ...), condition=%wide.region_9.10_spmd, body=%wide.region_8.9_spmd.sunk | while | flops 399362 | bytes 1613925 | solution.py:13
  143.8 3.2 copy.70
  147.0 55.0 %all-gather.14.cloned.1.call-done = bf16[128,4096]{0,1:T(8,128)(2,1)} async-done(((bf16[128,128]{0,1:T(8,128)(2,1)}), bf16[128,4096]{0,1:T(8,128)(2,1)}) %all-gather.14.cloned.1.call-update) | async-done | bytes 1048592 | tf_op jit(solution)/shard_map/all_gather | solution.py:186
  207.1 3.7 fusion.64
  210.8 98.0 %reduce-scatter.3.cloned.1.call-done = bf16[128,128]{1,0:T(8,128)(2,1)} async-done(((bf16[4096,128]{1,0:T(8,128)(2,1)}), bf16[128,128]{1,0:T(8,128)(2,1)}) %reduce-scatter.3.cloned.1.call-update) | async-done | bytes 32784 | tf_op jit(solution)/shard_map/reduce_scatter | solution.py:202
  309.6 3.2 collective-permute-start
  317.3 59.8 %all-gather.16.cloned.1.call-done = bf16[128,4096]{0,1:T(8,128)(2,1)} async-done(((bf16[128,128]{0,1:T(8,128)(2,1)}), bf16[128,4096]{0,1:T(8,128)(2,1)}) %all-gather.16.cloned.1.call-update) | async-done | bytes 1048592 | tf_op jit(solution)/shard_map/all_gather | solution.py:131
  378.9 4.4 fusion.73
  388.4 15.7 %all-gather.4 = f32[64,128]{1,0:T(8,128)S(1)} all-gather(f32[8,128]{1,0:T(8,128)} %get-tuple-element.185), channel_id=6, replica_groups=mesh['section'=16,'kv'=8,'tp'=4] {'kv'}, dimensions={0}, use_global_device_ids=true | all-gather | bytes 36864 | tf_op jit(solution)/shard_map/all_gather | solution.py:10
  404.2 12.8 %all-gather.5 = f32[64,128]{1,0:T(8,128)S(1)} all-gather(f32[8,128]{1,0:T(8,128)S(1)} %get-tuple-element.186), channel_id=7, replica_groups=mesh['section'=16,'kv'=8,'tp'=4] {'kv'}, dimensions={0}, use_global_device_ids=true | all-gather | bytes 36864 | tf_op jit(solution)/shard_map/all_gather | solution.py:10
  418.4 10.1 %all-gather.24.cloned.1.call-done = f32[64,128,128]{2,1,0:T(8,128)} async-done(((f32[8,128,128]{2,1,0:T(8,128)}), f32[64,128,128]{2,1,0:T(8,128)}) %all-gather.24.cloned.1.call-update) | async-done | bytes 4194320 | tf_op jit(solution)/shard_map/all_gather | solution.py:10
  428.6 4.3 slice.83
  432.9 10.9 %while.29 = (s32[]{:T(128)}, f32[8,128]{1,0:T(8,128)S(1)}, f32[8,128]{1,0:T(8,128)S(1)}, f32[8,128,128]{2,1,0:T(8,128)S(1)}, f32[7,8,128]{2,1,0:T(8,128)S(1)}, /...) while((s32[]{:T(128)}, f32[8,128]{1,0:T(8,128)S(1)}, f32[8,128]{1,0:T(8,128)S(1)}, ...), condition=%wide.region_21.22_spmd, body=%wide.region_20.21_spmd.sunk | while | flops 399362 | bytes 1613925 | solution.py:13
  444.8 58.2 %all-gather.18.cloned.1.call-done = bf16[128,4096]{0,1:T(8,128)(2,1)} async-done(((bf16[128,128]{0,1:T(8,128)(2,1)}), bf16[128,4096]{0,1:T(8,128)(2,1)}) %all-gather.18.cloned.1.call-update) | async-done | bytes 1048592 | tf_op jit(solution)/shard_map/all_gather | solution.py:186
  507.9 3.7 fusion.65
  511.7 98.1 %reduce-scatter.5.cloned.1.call-done = bf16[128,128]{1,0:T(8,128)(2,1)} async-done(((bf16[4096,128]{1,0:T(8,128)(2,1)}), bf16[128,128]{1,0:T(8,128)(2,1)}) %reduce-scatter.5.cloned.1.call-update) | async-done | bytes 32784 | tf_op jit(solution)/shard_map/reduce_scatter | solution.py:202
  610.5 3.2 collective-permute-start.1
  (163 shorter events, 71.2 us)
Async XLA Ops:
  7.2 199.9 %copy-start = (bf16[1,144,4096]{2,1,0:T(8,128)(2,1)S(1)}, bf16[1,144,4096]{2,1,0:T(8,128)(2,1)}, u32[]{:S(2)}) copy-start(bf16[1,144,4096]{2,1,0:T(8,128)(2,1)} %param.30) | copy-start | bytes 3538948
  7.2 68.4 %all-gather.20.cloned.1.call-start = ((), (), s32[]{:S(2)}) async-start(), calls=%async_computation.7 | async-start | bytes 1081344 | tf_op jit(solution)/shard_map/all_gather | solution.py:131
  8.8 118.7 %all-gather.22.cloned.1.call-start = ((), (), s32[]{:S(2)}) async-start(), calls=%async_computation.8 | async-start | bytes 4718592 | tf_op jit(solution)/shard_map/all_gather | solution.py:10
  12.4 71.1 %copy-start.5 = (bf16[64,8,128]{2,0,1:T(8,128)(2,1)}, bf16[64,8,128]{2,0,1:T(8,128)(2,1)S(1)}, u32[]{:S(2)}) copy-start(bf16[64,8,128]{2,0,1:T(8,128)(2,1)S(1)} %get-tuple-element.277) | copy-start | bytes 393220
  12.5 71.1 %copy-start.10 = (bf16[64,8,128]{2,0,1:T(8,128)(2,1)}, bf16[64,8,128]{2,0,1:T(8,128)(2,1)S(1)}, u32[]{:S(2)}) copy-start(bf16[64,8,128]{2,0,1:T(8,128)(2,1)S(1)} %get-tuple-element.278) | copy-start | bytes 393220
  80.7 35.5 %copy-start.8 = (bf16[128,4096]{0,1:T(8,128)(2,1)}, bf16[128,4096]{0,1:T(8,128)(2,1)S(1)}, u32[]{:S(2)}) copy-start(bf16[128,4096]{0,1:T(8,128)(2,1)S(1)} %get-tuple-element.270) | copy-start | bytes 3145732
  88.1 114.0 %all-gather.14.cloned.1.call-start = ((), (), s32[]{:S(2)}) async-start(), calls=%async_computation.2 | async-start | bytes 1081344 | tf_op jit(solution)/shard_map/all_gather | solution.py:186
  88.8 43.0 %copy-start.21 = (f32[128]{0:T(128)}, f32[128]{0:T(128)S(1)}, u32[]{:S(2)}) copy-start(f32[128]{0:T(128)S(1)} %multiply_exponential_fusion.1) | copy-start | bytes 1540
  143.8 165.1 %reduce-scatter.3.cloned.1.call-start = ((), (), s32[]{:S(2)}) async-start(), calls=%async_computation.3 | async-start | bytes 1081344 | tf_op jit(solution)/shard_map/reduce_scatter | solution.py:202
  147.0 60.1 %copy-start.1 = (bf16[1,144,2,4096]{3,1,2,0:T(8,128)(2,1)}, bf16[1,144,2,4096]{3,1,2,0:T(8,128)(2,1)S(1)}, u32[]{:S(2)}) copy-start(bf16[1,144,2,4096]{3,1,2,0:T(8,128)(2,1)S(1)} %copy.70) | copy-start | bytes 7077892
  210.8 168.1 %copy-start.18 = (f32[1,4096]{1,0:T(1,128)S(1)}, f32[1,4096]{1,0:T(1,128)}, u32[]{:S(2)}) copy-start(f32[1,4096]{1,0:T(1,128)} %param.24) | copy-start | bytes 49156
  210.8 168.1 %copy-start.19 = (f32[1,4096]{1,0:T(1,128)S(1)}, f32[1,4096]{1,0:T(1,128)}, u32[]{:S(2)}) copy-start(f32[1,4096]{1,0:T(1,128)} %param.23) | copy-start | bytes 49156
  210.8 166.3 %all-gather.16.cloned.1.call-start = ((), (), s32[]{:S(2)}) async-start(), calls=%async_computation.4 | async-start | bytes 1081344 | tf_op jit(solution)/shard_map/all_gather | solution.py:131
  309.6 7.0 %collective-permute-start = (bf16[128,128]{0,1:T(8,128)(2,1)S(1)}, bf16[128,128]{0,1:T(8,128)(2,1)S(1)}, u32[]{:S(2)}, u32[]{:S(2)}) collective-permute-start(bf16[128,128]{0,1:T(8,128)(2,1)S(1)} %fusion.121), channel_id=1, source_target_pairs={{0,32},{32,64},{64,96},{96,128},{128,160},{160,192},{192,224},{224... | collective-permute-start | bytes 98312 | tf_op jit(solution)/shard_map/ppermute | solution.py:19
  316.6 66.7 %copy-start.17 = (bf16[128,128]{0,1:T(8,128)(2,1)}, bf16[128,128]{0,1:T(8,128)(2,1)S(1)}, u32[]{:S(2)}) copy-start(bf16[128,128]{0,1:T(8,128)(2,1)S(1)} %collective-permute-done) | copy-start | bytes 98308
  317.3 111.3 %all-gather.24.cloned.1.call-start = ((), (), s32[]{:S(2)}) async-start(), calls=%async_computation.9 | async-start | bytes 4718592 | tf_op jit(solution)/shard_map/all_gather | solution.py:10
  383.3 33.9 %copy-start.7 = (bf16[128,4096]{0,1:T(8,128)(2,1)}, bf16[128,4096]{0,1:T(8,128)(2,1)S(1)}, u32[]{:S(2)}) copy-start(bf16[128,4096]{0,1:T(8,128)(2,1)S(1)} %get-tuple-element.268) | copy-start | bytes 3145732
  383.6 33.4 %copy-start.22 = (f32[128]{0:T(128)S(1)}, f32[128]{0:T(128)}, u32[]{:S(2)}) copy-start(f32[128]{0:T(128)} %copy-done.21) | copy-start | bytes 1540
  383.6 33.7 %copy-start.25 = (f32[128]{0:T(128)S(1)}, f32[128]{0:T(128)}, u32[]{:S(2)}) copy-start(f32[128]{0:T(128)} %copy-done.24) | copy-start | bytes 1540
  387.3 115.7 %all-gather.18.cloned.1.call-start = ((), (), s32[]{:S(2)}) async-start(), calls=%async_computation.5 | async-start | bytes 1081344 | tf_op jit(solution)/shard_map/all_gather | solution.py:186
  388.4 40.1 %copy-start.12 = (f32[128,128]{1,0:T(8,128)}, f32[128,128]{1,0:T(8,128)S(1)}, u32[]{:S(2)}) copy-start(f32[128,128]{1,0:T(8,128)S(1)} %fusion.88) | copy-start | bytes 196612
  444.8 63.1 %copy-start.2 = (bf16[1,144,2,4096]{3,1,2,0:T(8,128)(2,1)S(1)}, bf16[1,144,2,4096]{3,1,2,0:T(8,128)(2,1)}, u32[]{:S(2)}) copy-start(bf16[1,144,2,4096]{3,1,2,0:T(8,128)(2,1)} %copy-done.1) | copy-start | bytes 7077892
  444.8 165.0 %reduce-scatter.5.cloned.1.call-start = ((), (), s32[]{:S(2)}) async-start(), calls=%async_computation.6 | async-start | bytes 1081344 | tf_op jit(solution)/shard_map/reduce_scatter | solution.py:202
  610.5 7.0 %collective-permute-start.1 = (bf16[128,128]{0,1:T(8,128)(2,1)S(1)}, bf16[128,128]{0,1:T(8,128)(2,1)S(1)}, u32[]{:S(2)}, u32[]{:S(2)}) collective-permute-start(bf16[128,128]{0,1:T(8,128)(2,1)S(1)} %fusion.119), channel_id=1, source_target_pairs={{0,32},{32,64},{64,96},{96,128},{128,160},{160,192},{192,224},{224... | collective-permute-start | bytes 98312 | tf_op jit(solution)/shard_map/ppermute | solution.py:19
  (14 other events, 118.8 us)
Sparse Core Ops, SparseCore 0:
  11.7 63.8 all-gather.19
  88.2 39.2 all-gather.21
  143.9 58.1 all-gather.13
  210.9 97.8 reduce-scatter.2
  317.4 59.6 all-gather.15
  387.4 41.0 all-gather.23
  444.9 58.1 all-gather.17
  511.8 97.9 reduce-scatter.4
where the time goes:
time: 629 us; the launch traced here: 626 us
  waiting for transfers between devices  458 us (73%)
  blocking collectives  54.8 us (9%)
  other arithmetic  43.6 us (7%)
  matrix products  23.4 us (4%)
  local copies, waits for them, and re-layouts  22.9 us (4%)
  between operations  15.4 us (2%)
  starting transfers between devices  6.72 us (1%)
    reduce_scatter x2, waiting for transfers between devices, per_device(): lax.psum_scatter(lax.dot_general(weights_out, hidden_cols, (((0,), (0,)),...  196 us
    all_gather x2, waiting for transfers between devices, per_device(): assembled = lax.all_gather(incoming, ('kv', 'tp'), axis=1, tiled=True)  123 us
    all_gather x2, waiting for transfers between devices, per_device(): mixed_in = lax.all_gather(mixed_block, ('kv', 'tp'), axis=1, tiled=True)  113 us
    all_gather x4, blocking collectives, joined(): pieces = jax.tree.map(lambda part: lax.all_gather(part, axis), value)  54.8 us
    add x14, other arithmetic, join_partials(): first[2] * first_scale[..., None] + second[2] * second_scale[..., None]  21.3 us
    all_gather x2, waiting for transfers between devices, joined(): pieces = jax.tree.map(lambda part: lax.all_gather(part, axis), value)  21.1 us
  transfers between devices with their start and end apart: 10, of which 10 were waited for; matrix products, arithmetic and copies ran while one was open for 2% of the time, Pallas kernels for 0%

commit v1 on v0

v1 whole, which is shorter than its diff:
```python
import functools

import jax
import jax.numpy as jnp
from jax import lax
from jax.experimental import pallas as pl
from jax.experimental.pallas import tpu as pltpu
from jax.sharding import PartitionSpec as P

TICKS = 2
TOK = 128
HALF = 64
HEAD = 128
DIM = 4096
UNITS = 144
BLOCKS = 32
SHARDS = 8
ROWS = 64
EPS = 1e-6
SECTION = ("x", "core", "tp")
F32 = jnp.float32
BF16 = jnp.bfloat16
HIGH = lax.Precision.HIGHEST


def dot(left, right, dims, precision=None):
    return lax.dot_general(
        left, right, ((dims[:1], dims[1:]), ((), ())), precision=precision, preferred_element_type=F32
    )


def block_place():
    return (lax.axis_index("x") * 2 + lax.axis_index("core")) * 4 + lax.axis_index("tp")


def write_square_sums(rows, parts_ref):
    squares = rows.astype(F32)
    squares = squares * squares
    sums = dot(jnp.ones((8, HEAD), F32), squares, (1, 1), HIGH)
    parts_ref[...] = jnp.concatenate([sums] * (BLOCKS // 8), axis=0)


def first_squares_kernel(rows_ref, parts_ref):
    write_square_sums(rows_ref[...], parts_ref)


def later_squares_kernel(passed_ref, entering_ref, rows_ref, parts_ref):
    rows = jnp.where(lax.axis_index("section") == 0, entering_ref[...], passed_ref[...])
    rows_ref[...] = rows
    write_square_sums(rows, parts_ref)


def attention_kernel(
    tick,
    lengths_ref,
    decay_ref,
    rows_ref,
    parts_ref,
    gain_ref,
    key_gain_ref,
    linear_gain_ref,
    memory_ref,
    prefix_ref,
    past_ref,
    spread_ref,
    mixed_ref,
    new_memory_ref,
    turn_ref,
):
    scale = HEAD**-0.5
    place = pl.ds(pl.multiple_of(block_place() * HEAD, HEAD), HEAD)
    sums = dot(parts_ref[...], jnp.ones((BLOCKS, HEAD), F32), (0, 0), HIGH)
    rows = rows_ref[...].astype(F32)
    normed = rows * lax.rsqrt(sums * (1.0 / DIM) + EPS) * gain_ref[:, place]
    queries = normed.astype(BF16)
    keys = (normed * key_gain_ref[:, place]).astype(BF16)
    turn_ref[0] = keys
    turn_ref[1] = queries

    decay = decay_ref[0, 0]
    shape = (TOK, TOK)
    row = lax.broadcasted_iota(jnp.int32, shape, 0)
    column = lax.broadcasted_iota(jnp.int32, shape, 1)
    causal = column <= row
    own_scores = dot(queries, keys, (1, 1)) * scale
    age = jnp.where(causal, row - column, 0).astype(F32)
    weights = jnp.where(causal, own_scores * jnp.exp(-decay * age), 0.0).astype(BF16)
    row = row.astype(F32)
    memory = memory_ref[...]
    wide = queries.astype(F32)
    raw = dot(weights, queries, (1, 0)) + dot(wide, memory, (1, 0), HIGH) * jnp.exp(
        -decay * (row + 1.0)
    )
    tail = keys.astype(F32) * jnp.exp(-decay * (TOK - 1.0 - row))
    new_memory_ref[...] = memory * jnp.exp(jnp.full(shape, -decay * TOK, F32)) + (
        dot(tail, wide, (0, 0), HIGH) * scale
    )
    spread = jnp.mean(raw * raw, axis=1, keepdims=True)
    linear = raw * lax.rsqrt(spread + EPS) * linear_gain_ref[...]

    prefix_keys = prefix_ref[:, :ROWS, :].reshape(SHARDS * ROWS, HEAD)
    prefix_values = prefix_ref[:, ROWS:, :].reshape(SHARDS * ROWS, HEAD)
    slot = lax.broadcasted_iota(jnp.int32, (1, SHARDS * ROWS), 1)
    used = jnp.zeros((1, SHARDS * ROWS), jnp.int32)
    for shard in range(SHARDS):
        used = jnp.where(slot // ROWS == shard, lengths_ref[0, shard], used)
    prefix_scores = jnp.where(
        slot % ROWS < used, dot(queries, prefix_keys, (1, 1)) * scale, -1e30
    )
    groups = [
        (prefix_scores, prefix_values),
        (jnp.where(causal, own_scores, -1e30), queries),
    ]
    if tick:
        groups.append((dot(queries, past_ref[0], (1, 1)) * scale, past_ref[1]))
    top = functools.reduce(
        jnp.maximum, [jnp.max(scores, axis=1, keepdims=True) for scores, _ in groups]
    )
    total = 0.0
    weighted = 0.0
    for scores, values in groups:
        probabilities = jnp.exp(scores - top)
        total = total + jnp.sum(probabilities, axis=1, keepdims=True)
        weighted = weighted + dot(probabilities.astype(BF16), values, (1, 0))
    mixed = (rows + (linear + weighted / total)).astype(BF16)
    mixed_ref[...] = mixed
    for block in range(BLOCKS):
        half = block // 4 % 2
        spread_ref[block] = mixed[half * HALF : (half + 1) * HALF]


def feed_kernel(rows_ref, gain_ref, near_ref, far_ref, out_ref, feed_ref, wide_ref):
    squares = jnp.zeros((HALF, HEAD), F32)
    for block in range(BLOCKS):
        place = slice(block * HEAD, (block + 1) * HEAD)
        rows = rows_ref[block].astype(F32)
        squares = squares + rows * rows
        feed_ref[:, place] = (rows * gain_ref[:, place]).astype(BF16)
    sums = dot(jnp.ones((8, HEAD), F32), squares, (1, 1), HIGH)[:1]
    factor = lax.rsqrt(sums * (1.0 / DIM) + EPS)
    wide_ref[...] = jnp.zeros_like(wide_ref)
    step = 512

    @pl.loop(0, DIM // step)
    def _(chunk):
        place = pl.ds(pl.multiple_of(chunk * step, step), step)
        feed = feed_ref[:, place]
        for side, ref in enumerate((near_ref, far_ref)):
            wide_ref[side] += dot(ref[: 2 * UNITS, place], feed, (1, 1))

    hidden = []
    for side in range(2):
        gate = wide_ref[side, :UNITS] * factor
        up = wide_ref[side, UNITS:] * factor
        hidden.append((gate / (1.0 + jnp.exp(-gate)) * up).astype(BF16))

    for chunk in range(DIM // step):
        place = slice(chunk * step, (chunk + 1) * step)
        down = dot(hidden[0], near_ref[2 * UNITS :, place], (0, 0)) + dot(
            hidden[1], far_ref[2 * UNITS :, place], (0, 0)
        )
        for block in range(step // HEAD):
            out_ref[chunk * (step // HEAD) + block] = down[
                :, block * HEAD : (block + 1) * HEAD
            ].astype(BF16)


def finish_kernel(parts_ref, mixed_ref, out_ref):
    for half in range(2):
        total = jnp.zeros((HALF, HEAD), F32)
        for block in range(BLOCKS):
            if block // 4 % 2 == half:
                total = total + parts_ref[block].astype(F32)
        place = slice(half * HALF, (half + 1) * HALF)
        out_ref[place] = (mixed_ref[place].astype(F32) + total).astype(BF16)


def shape_of(*shape, dtype=BF16):
    return jax.ShapeDtypeStruct(shape, dtype)


def local_call(kernel, outs, ins, scratch=(), scalars=0):
    vmem = pl.BlockSpec(memory_space=pltpu.VMEM)
    smem = pl.BlockSpec(memory_space=pltpu.SMEM)
    return pl.pallas_call(
        kernel,
        out_shape=outs,
        in_specs=[smem] * scalars + [vmem] * (len(ins) - scalars),
        out_specs=jax.tree.map(lambda _: vmem, outs),
        scratch_shapes=list(scratch),
        compiler_params=pltpu.CompilerParams(vmem_limit_bytes=40 * 1024 * 1024),
    )(*ins)


def swapped(value):
    return lax.ppermute(value, "core", [(0, 1), (1, 0)])


def exchanged(value, axes=SECTION):
    return lax.all_to_all(value, axes, 0, 0, tiled=True)


def per_device(
    arriving,
    entering,
    gain_attention,
    gain_key,
    decay_rate,
    state_in,
    gain_linear,
    gain_feed,
    gate_up,
    down_weight,
    prefix_keys,
    prefix_values,
    lengths,
):
    weights = jnp.concatenate([gate_up[0, :, 0], gate_up[0, :, 1], down_weight[0]], axis=0)
    far_weights = swapped(weights)
    prefix = jnp.concatenate([prefix_keys[0], prefix_values[0]], axis=0)
    prefix = exchanged(jnp.transpose(prefix, (1, 0, 2)), ("x", "core"))
    rows = arriving[0]
    memory = state_in[0, 0]
    turn = None
    arrived = []
    for tick in range(TICKS):
        if tick == 0:
            parts = local_call(first_squares_kernel, shape_of(BLOCKS, HEAD, dtype=F32), (rows,))
        else:
            rows, parts = local_call(
                later_squares_kernel,
                (shape_of(TOK, HEAD), shape_of(BLOCKS, HEAD, dtype=F32)),
                (arrived[-1], entering[tick - 1]),
            )
        parts = exchanged(parts)
        past = jnp.zeros((2, 16, HEAD), BF16) if turn is None else turn
        spread, mixed, memory, turn = local_call(
            functools.partial(attention_kernel, tick),
            (
                shape_of(BLOCKS, HALF, HEAD),
                shape_of(TOK, HEAD),
                shape_of(HEAD, HEAD, dtype=F32),
                shape_of(2, TOK, HEAD),
            ),
            (
                lengths,
                decay_rate,
                rows,
                parts,
                gain_attention,
                gain_key,
                gain_linear,
                memory,
                prefix,
                past,
            ),
            scalars=2,
        )
        spread = exchanged(spread)
        down = local_call(
            feed_kernel,
            shape_of(BLOCKS, HALF, HEAD),
            (spread, gain_feed, weights, far_weights),
            scratch=(pltpu.VMEM((HALF, DIM), BF16), pltpu.VMEM((2, 2 * UNITS, HALF), F32)),
        )
        down = exchanged(down)
        finished = local_call(finish_kernel, shape_of(TOK, HEAD), (down, mixed))
        size = lax.axis_size("section")
        arrived.append(
            lax.ppermute(finished, "section", [(i, (i + 1) % size) for i in range(size)])
        )
    return (jnp.stack(arrived)[:, None], memory[None, None])


def solution(mesh):
    shape = mesh.devices.shape
    split = jax.sharding.Mesh(
        mesh.devices.reshape(shape[0], shape[1] // 2, 2, shape[2]), ("section", "x", "core", "tp")
    )
    kv = ("x", "core")
    in_specs = (
        P("section", None, SECTION),
        P(None, None, SECTION),
        P("section", None),
        P("section", None),
        P("section", SECTION),
        P("section", SECTION, None, None),
        P("section", SECTION),
        P("section", None),
        P("section", SECTION, None, None),
        P("section", SECTION, None),
        P("section", kv, None, "tp"),
        P("section", kv, None, "tp"),
        P("section", None),
    )
    out_specs = (P(None, "section", None, SECTION), P("section", SECTION, None, None))
    return jax.shard_map(
        per_device, mesh=split, in_specs=in_specs, out_specs=out_specs, check_vma=False
    )
```

time: 629 us -> 153 us (0.24)
  waiting for transfers between devices: 458 us -> 23.1 us
  other arithmetic: 43.6 us -> 1.79 us
  matrix products: 23.4 us -> 0 us
  blocking collectives: 54.8 us -> 72.7 us
  Pallas kernels: 0 us -> 15.3 us
  starting transfers between devices: 6.72 us -> 21.6 us
  between operations: 15.4 us -> 1.46 us
  local copies, waits for them, and re-layouts: 22.9 us -> 15.9 us
    all_gather x6 -> x0, waiting for transfers between devices: 257 us -> none  [the longest x2 123 us: per_device(): assembled = lax.all_gather(incoming, ('kv', 'tp'), axis=1, tiled=True)]
    reduce_scatter x2 -> x0, waiting for transfers between devices: 196 us -> none  [per_device(): lax.psum_scatter(lax.dot_general(weights_out, hidden_cols, (((0,), (0,)),...]
    all_to_all x0 -> x5, blocking collectives: none -> 72.7 us  [exchanged(): return lax.all_to_all(value, axes, 0, 0, tiled=True)]
    all_gather x4 -> x0, blocking collectives: 54.8 us -> none  [joined(): pieces = jax.tree.map(lambda part: lax.all_gather(part, axis), value)]
    dot_general x14 -> x0, matrix products: 23.4 us -> none  [the longest x2 7.45 us: per_device(): lax.dot_general(weights_out, hidden_cols, (((0,), (0,)), ((), ())), prefe...]
    add x28 -> x0, other arithmetic: 21.5 us -> none  [the longest x14 21.3 us: join_partials(): first[2] * first_scale[..., None] + second[2] * second_scale[..., None]]
    pallas_call x0 -> x8, Pallas kernels: none -> 15.3 us  [local_call(): pl.pallas_call(kernel, out_shape=outs, in_specs=[smem] * scalars + [vmem]...]
    all_to_all x0 -> x2, waiting for transfers between devices: none -> 10.9 us  [exchanged(): return lax.all_to_all(value, axes, 0, 0, tiled=True)]
  transfers between devices with their start and end apart: 10 -> 5, of which waited for: 10 -> 4; matrix products, arithmetic and copies ran while one was open for 2% -> 1% of each run, Pallas kernels for 0% -> 1%
where the time goes in v1:
time: 153 us; the launch traced here: 152 us
  blocking collectives  72.7 us (48%)
  waiting for transfers between devices  23.1 us (15%)
  starting transfers between devices  21.6 us (14%)
  local copies, waits for them, and re-layouts  15.9 us (10%)
  Pallas kernels  15.3 us (10%)
  other arithmetic  1.79 us (1%)
    all_to_all x5, blocking collectives, exchanged(): return lax.all_to_all(value, axes, 0, 0, tiled=True)  72.7 us
    pallas_call x8, Pallas kernels, local_call(): pl.pallas_call(kernel, out_shape=outs, in_specs=[smem] * scalars + [vmem]...  15.3 us
    ppermute x2, waiting for transfers between devices, per_device(): lax.ppermute(finished, 'section', [(i, (i + 1) % size) for i in range(siz...  12.2 us
    all_to_all x2, waiting for transfers between devices, exchanged(): return lax.all_to_all(value, axes, 0, 0, tiled=True)  10.9 us
    all_to_all x2, starting transfers between devices, exchanged(): return lax.all_to_all(value, axes, 0, 0, tiled=True)  9.01 us
    ppermute x1, starting transfers between devices, swapped(): return lax.ppermute(value, 'core', [(0, 1), (1, 0)])  8.79 us
    slice x1, local copies, waits for them, and re-layouts, per_device(): gate_up[0, :, 0]  7.2 us
    unnamed x30, local copies, waits for them, and re-layouts  5.02 us
  transfers between devices with their start and end apart: 5, of which 4 were waited for; matrix products, arithmetic and copies ran while one was open for 1% of the time, Pallas kernels for 1%

profile of v1, /device:TPU:1, one launch (start us, length us, event | category | flops | bytes accessed | tf_op | source)
XLA Modules:
  0.0 151.8 jit_solution(17743626894565814317)
XLA Ops:
  0.6 7.2 %fusion = (bf16[1,144,1,4096]{3,2,1,0:T(2,128)(2,1)S(1)}, bf16[1,144,1,4096]{3,2,1,0:T(2,128)(2,1)S(1)}) fusion(bf16[1,144,2,4096]{3,2,1,0:T(2,128)(2,1)} %param.21), kind=kLoop, calls=%fused_computation.7 | loop fusion | bytes 4718592 | tf_op jit(solution)/shard_map/slice | solution.py:218
  7.8 2.6 %copy_bitcast_fusion = (bf16[144,4096]{1,0:T(8,128)(2,1)S(1)}, bf16[144,4096]{1,0:T(8,128)(2,1)S(1)}) fusion(bf16[1,144,1,4096]{3,2,1,0:T(2,128)(2,1)S(1)} %get-tuple-element.25, bf16[1,144,1,4096]{3,2,1,0:T(2,128)(2,1)S(1)} %get-tuple-element.24), kind=kLoop, calls=%fused_computation.1 | loop fusion | bytes 4718592 | tf_op jit(solution)/shard_map/squeeze | solution.py:218
  10.9 8.8 %collective-permute-start = (bf16[432,4096]{1,0:T(8,128)(2,1)S(1)}, bf16[432,4096]{1,0:T(8,128)(2,1)}, u32[]{:S(2)}, u32[]{:S(2)}) collective-permute-start(bf16[432,4096]{1,0:T(8,128)(2,1)S(1)} %pad_maximum_fusion.near_ref), channel_id=1, source_target_pairs={{0,4},{4,0},{1,5},{5,1},{2,6},{6,2},{3,7},{7,3},{8,12},{12,8},{9,1... | collective-permute-start | bytes 10616840 | tf_op jit(solution)/shard_map/ppermute | solution.py:196
  20.6 4.3 %all-to-all-start = ((f32[32,1,128]{2,1,0:T(1,128)}), f32[32,1,128]{2,1,0:T(1,128)}, u32[]{:S(2)}, u32[]{:S(2)}) async-start(f32[32,1,128]{2,1,0:T(1,128)} %bitcast.34), calls=%async_computation | async-start | bytes 32768 | tf_op jit(solution)/shard_map/all_to_all | solution.py:200
  24.9 1.0 copy_bitcast_fusion.2
  26.6 4.9 %all-to-all-done = f32[32,1,128]{2,1,0:T(1,128)} async-done(((f32[32,1,128]{2,1,0:T(1,128)}), f32[32,1,128]{2,1,0:T(1,128)}, u32[]{:S(2)}, u32[]{:S(2)}) %all-to-all-start) | async-done | bytes 16416 | tf_op jit(solution)/shard_map/all_to_all | solution.py:200
  31.5 4.7 %all-to-all-start.1 = ((bf16[8,128,128]{2,1,0:T(8,128)(2,1)}), bf16[8,128,128]{2,1,0:T(8,128)(2,1)}, u32[]{:S(2)}, u32[]{:S(2)}) async-start(bf16[8,128,128]{2,1,0:T(8,128)(2,1)} %maximum_bitcast_fusion), calls=%async_computation.1 | async-start | bytes 524288 | tf_op jit(solution)/shard_map/all_to_all | solution.py:200
  36.9 6.0 %all-to-all-done.1.prefix_ref = bf16[8,128,128]{2,1,0:T(8,128)(2,1)} async-done(((bf16[8,128,128]{2,1,0:T(8,128)(2,1)}), bf16[8,128,128]{2,1,0:T(8,128)(2,1)}, u32[]{:S(2)}, u32[]{:S(2)}) %all-to-all-start.1) | async-done | bytes 262176 | tf_op jit(solution)/shard_map/all_to_all | solution.py:200
  42.9 0.8 copy-done.1
  43.6 0.8 copy-done.3
  45.2 0.7 copy-done.6
  47.2 1.9 %shard_map.141 = (bf16[32,64,128]{2,1,0:T(8,128)(2,1)S(1)}, bf16[128,128]{1,0:T(8,128)(2,1)S(1)}, f32[128,128]{1,0:T(8,128)S(1)}, bf16[2,128,128]{2,1,0:T(8,128)(2,1)S(1)}) custom-call(s32[1,8]{1,0:T(1,128)S(1)} %copy-done.10, f32[1,1]{1,0:T(1,128)S(6)} %copy.33.decay_ref, bf16[128,128]{1,0:T(8,128)(2,1)S(1)} %bitcast.30, f32[32,128]{1,0:T(8,128)} %bitcast.3.parts_ref, ...), custom_call_target="tpu_custom_call" | custom-call | tf_op jit(solution)/shard_map/pallas_call | solution.py:185
  49.1 15.1 %all_to_all.47.rows_ref = bf16[32,64,128]{2,1,0:T(8,128)(2,1)S(1)} all-to-all(bf16[32,64,128]{2,1,0:T(8,128)(2,1)S(1)} %get-tuple-element.11), channel_id=1, replica_groups=mesh['section'=16,'x'=4,'core'=2,'tp'=4] {'x','core','tp'}, dimensions={0} | all-to-all | bytes 1048576 | tf_op jit(solution)/shard_map/all_to_all | solution.py:200
  64.3 5.2 %shard_map.142 = bf16[32,64,128]{2,1,0:T(8,128)(2,1)S(1)} custom-call(bf16[32,64,128]{2,1,0:T(8,128)(2,1)S(1)} %all_to_all.47.rows_ref, f32[1,4096]{1,0:T(1,128)S(1)} %copy-done.2, bf16[432,4096]{1,0:T(8,128)(2,1)S(1)} %pad_maximum_fusion.near_ref, bf16[432,4096]{1,0:T(8,128)(2,1)} %collective-permute-done.far_ref), custom_call_target="tpu_custom_call" | custom-call | tf_op jit(solution)/shard_map/pallas_call | solution.py:185
  69.5 15.4 %all_to_all.48.parts_ref = bf16[32,64,128]{2,1,0:T(8,128)(2,1)S(1)} all-to-all(bf16[32,64,128]{2,1,0:T(8,128)(2,1)S(1)} %shard_map.142), channel_id=1, replica_groups=mesh['section'=16,'x'=4,'core'=2,'tp'=4] {'x','core','tp'}, dimensions={0} | all-to-all | bytes 1048576 | tf_op jit(solution)/shard_map/all_to_all | solution.py:200
  84.9 1.9 %collective-permute-start.1 = (bf16[128,128]{1,0:T(8,128)(2,1)S(1)}, bf16[128,128]{1,0:T(8,128)(2,1)S(1)}, u32[]{:S(2)}, u32[]{:S(2)}) collective-permute-start(bf16[128,128]{1,0:T(8,128)(2,1)S(1)} %shard_map.143), channel_id=1, source_target_pairs={{0,32},{32,64},{64,96},{96,128},{128,160},{160,192},{192,224},{224... | collective-permute-start | bytes 98312 | tf_op jit(solution)/shard_map/ppermute | solution.py:270
  86.9 8.2 %collective-permute-done.1.passed_ref = bf16[128,128]{1,0:T(8,128)(2,1)S(1)} collective-permute-done((bf16[128,128]{1,0:T(8,128)(2,1)S(1)}, bf16[128,128]{1,0:T(8,128)(2,1)S(1)}, u32[]{:S(2)}, u32[]{:S(2)}) %collective-permute-start.1) | collective-permute-done | bytes 32800 | tf_op jit(solution)/shard_map/ppermute | solution.py:270
  95.3 12.1 %all_to_all.49 = f32[32,1,128]{2,1,0:T(1,128)S(1)} all-to-all(f32[32,1,128]{2,1,0:T(1,128)S(1)} %bitcast.36), channel_id=1, replica_groups=mesh['section'=16,'x'=4,'core'=2,'tp'=4] {'x','core','tp'}, dimensions={0} | all-to-all | bytes 32768 | tf_op jit(solution)/shard_map/all_to_all | solution.py:200
  107.5 2.4 %shard_map.145 = (bf16[32,64,128]{2,1,0:T(8,128)(2,1)S(1)}, bf16[128,128]{1,0:T(8,128)(2,1)S(1)}, f32[128,128]{1,0:T(8,128)}, bf16[2,128,128]{2,1,0:T(8,128)(2,1)}) custom-call(s32[1,8]{1,0:T(1,128)S(1)} %copy-done.11, f32[1,1]{1,0:T(1,128)S(6)} %copy.33.decay_ref, bf16[128,128]{1,0:T(8,128)(2,1)S(1)} %get-tuple-element.13.rows_ref, f32[32,128]{1,0:T(8,128)S(1)} %bitcast.33, ...), custom_call_target="tpu_custom_call" | custom-call | tf_op jit(solution)/shard_map/pallas_call | solution.py:185
  109.9 14.8 %all_to_all.50.rows_ref = bf16[32,64,128]{2,1,0:T(8,128)(2,1)S(1)} all-to-all(bf16[32,64,128]{2,1,0:T(8,128)(2,1)S(1)} %get-tuple-element.17), channel_id=1, replica_groups=mesh['section'=16,'x'=4,'core'=2,'tp'=4] {'x','core','tp'}, dimensions={0} | all-to-all | bytes 1048576 | tf_op jit(solution)/shard_map/all_to_all | solution.py:200
  124.6 5.2 %shard_map.146 = bf16[32,64,128]{2,1,0:T(8,128)(2,1)S(1)} custom-call(bf16[32,64,128]{2,1,0:T(8,128)(2,1)S(1)} %all_to_all.50.rows_ref, f32[1,4096]{1,0:T(1,128)S(1)} %copy-done.2, bf16[432,4096]{1,0:T(8,128)(2,1)S(1)} %pad_maximum_fusion.near_ref, bf16[432,4096]{1,0:T(8,128)(2,1)} %collective-permute-done.far_ref), custom_call_target="tpu_custom_call" | custom-call | tf_op jit(solution)/shard_map/pallas_call | solution.py:185
  129.9 15.4 %all_to_all.51.parts_ref = bf16[32,64,128]{2,1,0:T(8,128)(2,1)S(1)} all-to-all(bf16[32,64,128]{2,1,0:T(8,128)(2,1)S(1)} %shard_map.146), channel_id=1, replica_groups=mesh['section'=16,'x'=4,'core'=2,'tp'=4] {'x','core','tp'}, dimensions={0} | all-to-all | bytes 1048576 | tf_op jit(solution)/shard_map/all_to_all | solution.py:200
  145.3 1.9 %collective-permute-start.2 = (bf16[128,128]{1,0:T(8,128)(2,1)S(1)}, bf16[128,128]{1,0:T(8,128)(2,1)S(1)}, u32[]{:S(2)}, u32[]{:S(2)}) collective-permute-start(bf16[128,128]{1,0:T(8,128)(2,1)S(1)} %shard_map.147), channel_id=1, source_target_pairs={{0,32},{32,64},{64,96},{96,128},{128,160},{160,192},{192,224},{224... | collective-permute-start | bytes 98312 | tf_op jit(solution)/shard_map/ppermute | solution.py:270
  147.2 3.9 %collective-permute-done.2 = bf16[128,128]{1,0:T(8,128)(2,1)S(1)} collective-permute-done((bf16[128,128]{1,0:T(8,128)(2,1)S(1)}, bf16[128,128]{1,0:T(8,128)(2,1)S(1)}, u32[]{:S(2)}, u32[]{:S(2)}) %collective-permute-start.2) | collective-permute-done | bytes 32800 | tf_op jit(solution)/shard_map/ppermute | solution.py:270
  (36 shorter events, 5.0 us)
Async XLA Ops:
  7.8 2.6 %copy-start.14 = (bf16[1,144,4096]{2,1,0:T(8,128)(2,1)S(1)}, bf16[1,144,4096]{2,1,0:T(8,128)(2,1)}, u32[]{:S(2)}) copy-start(bf16[1,144,4096]{2,1,0:T(8,128)(2,1)} %param.22) | copy-start | bytes 3538948
  10.5 9.3 %copy-start = (bf16[1,128,128]{2,1,0:T(8,128)(2,1)S(1)}, bf16[1,128,128]{2,1,0:T(8,128)(2,1)}, u32[]{:S(2)}) copy-start(bf16[1,128,128]{2,1,0:T(8,128)(2,1)} %param.13) | copy-start | bytes 98308
  10.9 53.3 %copy-start.2 = (f32[1,4096]{1,0:T(1,128)S(1)}, f32[1,4096]{1,0:T(1,128)}, u32[]{:S(2)}) copy-start(f32[1,4096]{1,0:T(1,128)} %gain_ref.7) | copy-start | bytes 49156
  10.9 53.3 %collective-permute-start = (bf16[432,4096]{1,0:T(8,128)(2,1)S(1)}, bf16[432,4096]{1,0:T(8,128)(2,1)}, u32[]{:S(2)}, u32[]{:S(2)}) collective-permute-start(bf16[432,4096]{1,0:T(8,128)(2,1)S(1)} %pad_maximum_fusion.near_ref), channel_id=1, source_target_pairs={{0,4},{4,0},{1,5},{5,1},{2,6},{6,2},{3,7},{7,3},{8,12},{12,8},{9,1... | collective-permute-start | bytes 10616840 | tf_op jit(solution)/shard_map/ppermute | solution.py:196
  19.9 0.6 copy-start.8
  20.6 11.0 %all-to-all-start = ((f32[32,1,128]{2,1,0:T(1,128)}), f32[32,1,128]{2,1,0:T(1,128)}, u32[]{:S(2)}, u32[]{:S(2)}) async-start(f32[32,1,128]{2,1,0:T(1,128)} %bitcast.34), calls=%async_computation | async-start | bytes 32768 | tf_op jit(solution)/shard_map/all_to_all | solution.py:200
  31.5 11.3 %all-to-all-start.1 = ((bf16[8,128,128]{2,1,0:T(8,128)(2,1)}), bf16[8,128,128]{2,1,0:T(8,128)(2,1)}, u32[]{:S(2)}, u32[]{:S(2)}) async-start(bf16[8,128,128]{2,1,0:T(8,128)(2,1)} %maximum_bitcast_fusion), calls=%async_computation.1 | async-start | bytes 524288 | tf_op jit(solution)/shard_map/all_to_all | solution.py:200
  42.9 0.8 copy-start.1
  43.6 0.8 copy-start.3
  44.5 0.7 copy-start.4
  45.2 0.7 copy-start.6
  45.9 0.7 copy-start.10
  46.6 0.7 copy-start.12
  64.2 30.9 %copy-start.9 = (bf16[1,128,128]{2,1,0:T(8,128)(2,1)S(1)}, bf16[1,128,128]{2,1,0:T(8,128)(2,1)}, u32[]{:S(2)}) copy-start(bf16[1,128,128]{2,1,0:T(8,128)(2,1)} %param.14) | copy-start | bytes 98308
  64.2 43.2 %copy-start.5 = (f32[1,4096]{1,0:T(1,128)S(1)}, f32[1,4096]{1,0:T(1,128)}, u32[]{:S(2)}) copy-start(f32[1,4096]{1,0:T(1,128)} %gain_ref.6) | copy-start | bytes 49156
  64.2 43.2 %copy-start.7 = (f32[1,4096]{1,0:T(1,128)S(1)}, f32[1,4096]{1,0:T(1,128)}, u32[]{:S(2)}) copy-start(f32[1,4096]{1,0:T(1,128)} %key_gain_ref.3) | copy-start | bytes 49156
  64.2 43.2 %copy-start.11 = (s32[1,8]{1,0:T(1,128)S(1)}, s32[1,8]{1,0:T(1,128)}, u32[]{:S(2)}) copy-start(s32[1,8]{1,0:T(1,128)} %lengths_ref.3) | copy-start | bytes 100
  64.2 43.2 %copy-start.13 = (f32[1,128]{1,0:T(1,128)S(1)}, f32[1,128]{1,0:T(1,128)}, u32[]{:S(2)}) copy-start(f32[1,128]{1,0:T(1,128)} %linear_gain_ref.3) | copy-start | bytes 1540
  84.9 10.2 %collective-permute-start.1 = (bf16[128,128]{1,0:T(8,128)(2,1)S(1)}, bf16[128,128]{1,0:T(8,128)(2,1)S(1)}, u32[]{:S(2)}, u32[]{:S(2)}) collective-permute-start(bf16[128,128]{1,0:T(8,128)(2,1)S(1)} %shard_map.143), channel_id=1, source_target_pairs={{0,32},{32,64},{64,96},{96,128},{128,160},{160,192},{192,224},{224... | collective-permute-start | bytes 98312 | tf_op jit(solution)/shard_map/ppermute | solution.py:270
  145.3 5.9 %collective-permute-start.2 = (bf16[128,128]{1,0:T(8,128)(2,1)S(1)}, bf16[128,128]{1,0:T(8,128)(2,1)S(1)}, u32[]{:S(2)}, u32[]{:S(2)}) collective-permute-start(bf16[128,128]{1,0:T(8,128)(2,1)S(1)} %shard_map.147), channel_id=1, source_target_pairs={{0,32},{32,64},{64,96},{96,128},{128,160},{160,192},{192,224},{224... | collective-permute-start | bytes 98312 | tf_op jit(solution)/shard_map/ppermute | solution.py:270

commit v2 on v1

v2 whole, which is shorter than its diff:
```python
import functools

import jax
import jax.numpy as jnp
from jax import lax
from jax.experimental import pallas as pl
from jax.experimental.pallas import tpu as pltpu
from jax.sharding import PartitionSpec as P

TICKS = 2
TOK = 128
HALF = 64
HEAD = 128
DIM = 4096
UNITS = 144
BLOCKS = 32
SHARDS = 8
ROWS = 64
GROUPS = 3
GROUP = UNITS // GROUPS
EPS = 1e-6
MASKED = -1e30
SECTION = ("x", "core", "tp")
F32 = jnp.float32
BF16 = jnp.bfloat16
HIGH = lax.Precision.HIGHEST


def dot(left, right, dims, precision=None):
    return lax.dot_general(
        left, right, ((dims[:1], dims[1:]), ((), ())), precision=precision, preferred_element_type=F32
    )


def block_place():
    return (lax.axis_index("x") * 2 + lax.axis_index("core")) * 4 + lax.axis_index("tp")


def write_square_sums(rows, parts_ref):
    squares = rows.astype(F32)
    squares = squares * squares
    sums = dot(jnp.ones((8, HEAD), F32), squares, (1, 1), HIGH)
    parts_ref[...] = jnp.concatenate([sums] * (BLOCKS // 8), axis=0)


def first_squares_kernel(rows_ref, parts_ref):
    write_square_sums(rows_ref[...], parts_ref)


def later_squares_kernel(passed_ref, entering_ref, rows_ref, parts_ref):
    rows = jnp.where(lax.axis_index("section") == 0, entering_ref[...], passed_ref[...])
    rows_ref[...] = rows
    write_square_sums(rows, parts_ref)


def attention_kernel(tick, decay_ref, parts_in, prefix_in, rows_in, memory_in, *refs):
    scale = HEAD**-0.5
    place = pl.ds(pl.multiple_of(block_place() * HEAD, HEAD), HEAD)
    if tick == 0:
        lengths_hbm, gain_hbm, key_gain_hbm, linear_gain_hbm = refs[:4]
        spread_ref, mixed_ref, new_memory_ref, turn_ref, consts_ref, prefix_ref = refs[4:10]
        lengths_ref, gains_ref, parts_ref, rows_ref, memory_ref, sems = refs[10:]
        copies = [
            (parts_in, parts_ref),
            (rows_in, rows_ref),
            (gain_hbm.at[:, place], gains_ref.at[0]),
            (key_gain_hbm.at[:, place], gains_ref.at[1]),
            (linear_gain_hbm, gains_ref.at[2]),
            (memory_in, memory_ref),
            (lengths_hbm, lengths_ref),
            (prefix_in, prefix_ref),
        ]
        copies = [pltpu.make_async_copy(*pair, sems.at[i]) for i, pair in enumerate(copies)]
        for copy in copies:
            copy.start()
        for copy in copies[:-1]:
            copy.wait()
        slot = lax.broadcasted_iota(jnp.int32, (1, SHARDS * ROWS), 1)
        used = jnp.zeros((1, SHARDS * ROWS), jnp.int32)
        for shard in range(SHARDS):
            used = jnp.where(slot // ROWS == shard, lengths_ref[0, shard], used)
        barred = jnp.where(slot % ROWS < used, 0.0, MASKED)
        consts_ref[0:1] = barred
        gain, key_gain, linear_gain = [gains_ref[index] for index in range(3)]
        for index in range(3):
            consts_ref[1:2, index * HEAD : (index + 1) * HEAD] = gains_ref[index]
    else:
        past_ref, consts_ref, spread_ref, mixed_ref, new_memory_ref, turn_ref = refs
        parts_ref, prefix_ref, rows_ref, memory_ref = parts_in, prefix_in, rows_in, memory_in
        barred = consts_ref[0:1]
        gain, key_gain, linear_gain = [
            consts_ref[1:2, index * HEAD : (index + 1) * HEAD] for index in range(3)
        ]
    decay = decay_ref[0, 0]
    sums = dot(parts_ref[...], jnp.ones((BLOCKS, HEAD), F32), (0, 0), HIGH)
    rows = rows_ref[...].astype(F32)
    normed = rows * lax.rsqrt(sums * (1.0 / DIM) + EPS) * gain
    queries = normed.astype(BF16)
    keys = (normed * key_gain).astype(BF16)
    turn_ref[0] = keys
    turn_ref[1] = queries

    shape = (TOK, TOK)
    row = lax.broadcasted_iota(jnp.int32, shape, 0)
    column = lax.broadcasted_iota(jnp.int32, shape, 1)
    causal = column <= row
    own_scores = dot(queries, keys, (1, 1)) * scale
    age = jnp.where(causal, row - column, 0).astype(F32)
    weights = jnp.where(causal, own_scores * jnp.exp(-decay * age), 0.0).astype(BF16)
    row = row.astype(F32)
    memory = memory_ref[...]
    wide = queries.astype(F32)
    raw = dot(weights, queries, (1, 0)) + dot(wide, memory, (1, 0), HIGH) * jnp.exp(
        -decay * (row + 1.0)
    )
    tail = keys.astype(F32) * jnp.exp(-decay * (TOK - 1.0 - row))
    new_memory_ref[...] = memory * jnp.exp(jnp.full(shape, -decay * TOK, F32)) + (
        dot(tail, wide, (0, 0), HIGH) * scale
    )
    spread = jnp.mean(raw * raw, axis=1, keepdims=True)
    linear = raw * lax.rsqrt(spread + EPS) * linear_gain

    if tick == 0:
        copies[-1].wait()
    prefix_keys = prefix_ref[:, :ROWS, :].reshape(SHARDS * ROWS, HEAD)
    prefix_values = prefix_ref[:, ROWS:, :].reshape(SHARDS * ROWS, HEAD)
    prefix_scores = dot(queries, prefix_keys, (1, 1)) * scale + barred
    groups = [
        (prefix_scores, prefix_values),
        (jnp.where(causal, own_scores, MASKED), queries),
    ]
    if tick:
        groups.append((dot(queries, past_ref[0], (1, 1)) * scale, past_ref[1]))
    top = functools.reduce(
        jnp.maximum, [jnp.max(scores, axis=1, keepdims=True) for scores, _ in groups]
    )
    total = 0.0
    weighted = 0.0
    for scores, values in groups:
        probabilities = jnp.exp(scores - top)
        total = total + jnp.sum(probabilities, axis=1, keepdims=True)
        weighted = weighted + dot(probabilities.astype(BF16), values, (1, 0))
    mixed = (rows + (linear + weighted / total)).astype(BF16)
    mixed_ref[...] = mixed
    for block in range(BLOCKS):
        half = block // 4 % 2
        spread_ref[block] = mixed[half * HALF : (half + 1) * HALF]


def feed_kernel(rows_ref, gain_ref, near_ref, far_ref, out_ref, wide_ref):
    step = 1024
    squares = jnp.zeros((HALF, HEAD), F32)
    sums = [0.0, 0.0]
    for first in range(0, DIM, step):
        place = slice(first, first + step)
        pieces = []
        for block in range(first // HEAD, (first + step) // HEAD):
            rows = rows_ref[block].astype(F32)
            squares = squares + rows * rows
            gain = gain_ref[:, block * HEAD : (block + 1) * HEAD]
            pieces.append((rows * gain).astype(BF16))
        feed = jnp.concatenate(pieces, axis=1)
        for side, ref in enumerate((near_ref, far_ref)):
            sums[side] = sums[side] + dot(ref[: 2 * UNITS, place], feed, (1, 1))
    mean = dot(jnp.ones((8, HEAD), F32), squares, (1, 1), HIGH)[:1] * (1.0 / DIM)
    factor = lax.rsqrt(mean + EPS)
    hidden = []
    for side in range(2):
        wide_ref[side] = sums[side]
        gate = wide_ref[side, pl.ds(0, UNITS, stride=2), :] * factor
        up = wide_ref[side, pl.ds(1, UNITS, stride=2), :] * factor
        hidden.append(jnp.transpose((gate / (1.0 + jnp.exp(-gate)) * up).astype(BF16)))
    for first in range(0, DIM, step):
        place = slice(first, first + step)
        down = dot(hidden[0], near_ref[2 * UNITS :, place], (1, 0)) + dot(
            hidden[1], far_ref[2 * UNITS :, place], (1, 0)
        )
        for block in range(step // HEAD):
            out_ref[first // HEAD + block] = down[:, block * HEAD : (block + 1) * HEAD].astype(BF16)


def prepare_kernel(gate_up_hbm, down_hbm, weights_ref, raw_ref, sems):
    copies = []
    for group in range(GROUPS):
        span = pl.ds(group * GROUP, GROUP)
        copies.append((gate_up_hbm.at[span], raw_ref.at[span]))
    copies.append((down_hbm, weights_ref.at[pl.ds(2 * UNITS, UNITS)]))
    copies = [pltpu.make_async_copy(*pair, sems.at[i]) for i, pair in enumerate(copies)]
    for copy in copies:
        copy.start()
    for group in range(GROUPS):
        copies[group].wait()

        @pl.loop(0, GROUP // 16)
        def _(part):
            raw = raw_ref[pl.ds(group * GROUP + part * 16, 16)]
            target = pl.ds(pl.multiple_of(2 * group * GROUP + part * 32, 32), 32)
            weights_ref[target] = raw.reshape(32, DIM)

    copies[GROUPS].wait()


def finish_kernel(parts_ref, mixed_ref, out_ref):
    for half in range(2):
        total = jnp.zeros((HALF, HEAD), F32)
        for block in range(BLOCKS):
            if block // 4 % 2 == half:
                total = total + parts_ref[block].astype(F32)
        place = slice(half * HALF, (half + 1) * HALF)
        out_ref[place] = (mixed_ref[place].astype(F32) + total).astype(BF16)


def shape_of(*shape, dtype=BF16):
    return jax.ShapeDtypeStruct(shape, dtype)


def local_call(kernel, outs, ins, scratch=(), spaces=None, cost=None, mib=8):
    spaces = spaces or {}
    ins = [
        pltpu.with_memory_space_constraint(value, spaces[i])
        if spaces.get(i) in (pltpu.HBM, pltpu.VMEM)
        else value
        for i, value in enumerate(ins)
    ]
    return pl.pallas_call(
        kernel,
        out_shape=outs,
        in_specs=[pl.BlockSpec(memory_space=spaces.get(i, pltpu.VMEM)) for i in range(len(ins))],
        out_specs=jax.tree.map(lambda _: pl.BlockSpec(memory_space=pltpu.VMEM), outs),
        scratch_shapes=list(scratch),
        compiler_params=pltpu.CompilerParams(vmem_limit_bytes=mib << 20),
        cost_estimate=cost,
    )(*ins)


def swapped(value):
    return lax.ppermute(value, "core", [(0, 1), (1, 0)])


def exchanged(value, axes=SECTION):
    return lax.all_to_all(value, axes, 0, 0, tiled=True)


def per_device(
    arriving,
    entering,
    gain_attention,
    gain_key,
    decay_rate,
    state_in,
    gain_linear,
    gain_feed,
    gate_up,
    down_weight,
    prefix_keys,
    prefix_values,
    lengths,
):
    rows = arriving[0]
    parts = local_call(first_squares_kernel, shape_of(BLOCKS, HEAD, dtype=F32), (rows,))
    weights = local_call(
        prepare_kernel,
        shape_of(3 * UNITS, DIM),
        (gate_up[0], down_weight[0]),
        scratch=(pltpu.VMEM((UNITS, 2, DIM), BF16), pltpu.SemaphoreType.DMA((GROUPS + 1,))),
        spaces=dict.fromkeys(range(2), pltpu.HBM),
        cost=pl.CostEstimate(flops=0, bytes_accessed=8 << 20, transcendentals=0),
        mib=16,
    )
    prefix = jnp.concatenate([prefix_keys[0], prefix_values[0]], axis=0)
    prefix = jnp.transpose(prefix, (1, 0, 2))
    parts = exchanged(parts)
    prefix, parts = lax.optimization_barrier((prefix, parts))
    prefix = exchanged(prefix, ("x", "core"))
    prefix, sent_weights = lax.optimization_barrier((prefix, weights))
    far_weights = swapped(sent_weights)
    memory = state_in[0, 0]
    arrived = []
    for tick in range(TICKS):
        if tick:
            rows, parts = local_call(
                later_squares_kernel,
                (shape_of(TOK, HEAD), shape_of(BLOCKS, HEAD, dtype=F32)),
                (arrived[-1], entering[tick - 1]),
            )
            parts = exchanged(parts)
        outs = (
            shape_of(BLOCKS, HALF, HEAD),
            shape_of(TOK, HEAD),
            shape_of(HEAD, HEAD, dtype=F32),
            shape_of(2, TOK, HEAD),
        )
        ins = (decay_rate, parts, prefix, rows, memory)
        kernel = functools.partial(attention_kernel, tick)
        if tick == 0:
            spread, mixed, memory, turn, consts, prefix = local_call(
                kernel,
                (
                    *outs,
                    shape_of(8, SHARDS * ROWS, dtype=F32),
                    shape_of(SHARDS, 2 * ROWS, HEAD),
                ),
                (*ins, lengths, gain_attention, gain_key, gain_linear),
                scratch=(
                    pltpu.SMEM((1, SHARDS), jnp.int32),
                    pltpu.VMEM((3, 1, HEAD), F32),
                    pltpu.VMEM((BLOCKS, HEAD), F32),
                    pltpu.VMEM((TOK, HEAD), BF16),
                    pltpu.VMEM((HEAD, HEAD), F32),
                    pltpu.SemaphoreType.DMA((8,)),
                ),
                spaces={0: pltpu.SMEM, **dict.fromkeys(range(1, 9), pltpu.HBM)},
            )
        else:
            spread, mixed, memory, turn = local_call(
                kernel, outs, (*ins, turn, consts), spaces={0: pltpu.SMEM}
            )
        spread = exchanged(spread)
        down = local_call(
            feed_kernel,
            shape_of(BLOCKS, HALF, HEAD),
            (spread, gain_feed, weights, far_weights),
            scratch=(pltpu.VMEM((2, 2 * UNITS, HALF), F32),),
            mib=16,
        )
        down = exchanged(down)
        finished = local_call(finish_kernel, shape_of(TOK, HEAD), (down, mixed))
        size = lax.axis_size("section")
        arrived.append(
            lax.ppermute(finished, "section", [(i, (i + 1) % size) for i in range(size)])
        )
    return (jnp.stack(arrived)[:, None], memory[None, None])


def solution(mesh):
    shape = mesh.devices.shape
    split = jax.sharding.Mesh(
        mesh.devices.reshape(shape[0], shape[1] // 2, 2, shape[2]), ("section", "x", "core", "tp")
    )
    kv = ("x", "core")
    in_specs = (
        P("section", None, SECTION),
        P(None, None, SECTION),
        P("section", None),
        P("section", None),
        P("section", SECTION),
        P("section", SECTION, None, None),
        P("section", SECTION),
        P("section", None),
        P("section", SECTION, None, None),
        P("section", SECTION, None),
        P("section", kv, None, "tp"),
        P("section", kv, None, "tp"),
        P("section", None),
    )
    out_specs = (P(None, "section", None, SECTION), P("section", SECTION, None, None))
    return jax.shard_map(
        per_device, mesh=split, in_specs=in_specs, out_specs=out_specs, check_vma=False
    )
```

time: 153 us -> 132 us (0.86)
  local copies, waits for them, and re-layouts: 15.9 us -> 1.78 us
  Pallas kernels: 15.3 us -> 10.9 us
    slice x1 -> x0, local copies, waits for them, and re-layouts: 7.2 us -> none  [per_device(): gate_up[0, :, 0]]
    all_to_all x2, starting transfers between devices: 9.01 us -> 15 us  [exchanged(): return lax.all_to_all(value, axes, 0, 0, tiled=True)]
    ppermute x1, starting transfers between devices: 8.79 us -> 2.94 us  [swapped(): return lax.ppermute(value, 'core', [(0, 1), (1, 0)])]
    pallas_call x8 -> x9, Pallas kernels: 15.3 us -> 10.9 us  [local_call(): pl.pallas_call(kernel, out_shape=outs, in_specs=[pl.BlockSpec(memory_spac...]
    unnamed x30 -> x8, local copies, waits for them, and re-layouts: 5.02 us -> 0.76 us
    squeeze x1 -> x0, local copies, waits for them, and re-layouts: 2.62 us -> none  [per_device(): gate_up[0, :, 1]]
  transfers between devices with their start and end apart: 5 -> 5, of which waited for: 4 -> 4; matrix products, arithmetic and copies ran while one was open for 1% -> 1% of each run, Pallas kernels for 1% -> 3%
where the time goes in v2:
time: 132 us; the launch traced here: 131 us
  blocking collectives  71.8 us (54%)
  waiting for transfers between devices  22.3 us (17%)
  starting transfers between devices  21.7 us (16%)
  Pallas kernels  10.9 us (8%)
  local copies, waits for them, and re-layouts  1.78 us (1%)
  between operations  1.37 us (1%)
  other arithmetic  1.36 us (1%)
    all_to_all x5, blocking collectives, exchanged(): return lax.all_to_all(value, axes, 0, 0, tiled=True)  71.8 us
    all_to_all x2, starting transfers between devices, exchanged(): return lax.all_to_all(value, axes, 0, 0, tiled=True)  15 us
    ppermute x2, waiting for transfers between devices, per_device(): lax.ppermute(finished, 'section', [(i, (i + 1) % size) for i in range(siz...  12.6 us
    pallas_call x9, Pallas kernels, local_call(): pl.pallas_call(kernel, out_shape=outs, in_specs=[pl.BlockSpec(memory_spac...  10.9 us
    all_to_all x2, waiting for transfers between devices, exchanged(): return lax.all_to_all(value, axes, 0, 0, tiled=True)  9.78 us
    ppermute x2, starting transfers between devices, per_device(): lax.ppermute(finished, 'section', [(i, (i + 1) % size) for i in range(siz...  3.84 us
    ppermute x1, starting transfers between devices, swapped(): return lax.ppermute(value, 'core', [(0, 1), (1, 0)])  2.94 us
  transfers between devices with their start and end apart: 5, of which 4 were waited for; matrix products, arithmetic and copies ran while one was open for 1% of the time, Pallas kernels for 3%

profile of v2, /device:TPU:1, one launch (start us, length us, event | category | flops | bytes accessed | tf_op | source)
XLA Modules:
  0.0 131.2 jit_solution(6880553424878685611)
XLA Ops:
  0.6 0.7 copy-done
  1.4 0.8 shard_map.140
  2.2 10.4 %all-to-all-start = ((f32[32,1,128]{2,1,0:T(1,128)}), f32[32,1,128]{2,1,0:T(1,128)S(1)}, u32[]{:S(2)}, u32[]{:S(2)}) async-start(f32[32,1,128]{2,1,0:T(1,128)} %bitcast.5), calls=%async_computation | async-start | bytes 32768 | tf_op jit(solution)/shard_map/all_to_all | solution.py:241
  12.6 1.0 copy_bitcast_fusion
  13.6 0.7 maximum_bitcast_fusion
  14.3 5.2 %all-to-all-done = f32[32,1,128]{2,1,0:T(1,128)S(1)} async-done(((f32[32,1,128]{2,1,0:T(1,128)}), f32[32,1,128]{2,1,0:T(1,128)S(1)}, u32[]{:S(2)}, u32[]{:S(2)}) %all-to-all-start) | async-done | bytes 16416 | tf_op jit(solution)/shard_map/all_to_all | solution.py:241
  19.5 4.6 %all-to-all-start.1 = ((bf16[8,128,128]{2,1,0:T(8,128)(2,1)}), bf16[8,128,128]{2,1,0:T(8,128)(2,1)}, u32[]{:S(2)}, u32[]{:S(2)}) async-start(bf16[8,128,128]{2,1,0:T(8,128)(2,1)} %maximum_bitcast_fusion), calls=%async_computation.1 | async-start | bytes 524288 | tf_op jit(solution)/shard_map/all_to_all | solution.py:241
  24.1 2.0 %shard_map.141.near_ref = bf16[432,4096]{1,0:T(8,128)(2,1)S(1)} custom-call(bf16[144,2,4096]{2,1,0:T(2,128)(2,1)} %bitcast.32, bf16[144,4096]{1,0:T(8,128)(2,1)} %bitcast.33), custom_call_target="tpu_custom_call" | custom-call | bytes 8388608 | tf_op jit(solution)/shard_map/pallas_call | solution.py:225
  26.1 4.6 %all-to-all-done.1.prefix_in = bf16[8,128,128]{2,1,0:T(8,128)(2,1)} async-done(((bf16[8,128,128]{2,1,0:T(8,128)(2,1)}), bf16[8,128,128]{2,1,0:T(8,128)(2,1)}, u32[]{:S(2)}, u32[]{:S(2)}) %all-to-all-start.1) | async-done | bytes 262176 | tf_op jit(solution)/shard_map/all_to_all | solution.py:241
  30.7 2.9 %collective-permute-start = (bf16[432,4096]{1,0:T(8,128)(2,1)S(1)}, bf16[432,4096]{1,0:T(8,128)(2,1)S(1)}, u32[]{:S(2)}, u32[]{:S(2)}) collective-permute-start(bf16[432,4096]{1,0:T(8,128)(2,1)S(1)} %shard_map.141.near_ref), channel_id=1, source_target_pairs={{0,4},{4,0},{1,5},{5,1},{2,6},{6,2},{3,7},{7,3},{8,12},{12,8},{9,1... | collective-permute-start | bytes 10616840 | tf_op jit(solution)/shard_map/ppermute | solution.py:237
  34.3 2.2 %shard_map.142 = (bf16[32,64,128]{2,1,0:T(8,128)(2,1)S(1)}, bf16[128,128]{1,0:T(8,128)(2,1)S(1)}, f32[128,128]{1,0:T(8,128)S(1)}, bf16[2,128,128]{2,1,0:T(8,128)...) custom-call(f32[1,1]{1,0:T(1,128)S(6)} %copy.25.decay_ref, f32[32,128]{1,0:T(8,128)} %bitcast.35, ...), custom_call_target="tpu_custom_call" | custom-call | tf_op jit(solution)/shard_map/pallas_call | solution.py:225
  36.5 14.2 %all_to_all.48.rows_ref = bf16[32,64,128]{2,1,0:T(8,128)(2,1)S(1)} all-to-all(bf16[32,64,128]{2,1,0:T(8,128)(2,1)S(1)} %get-tuple-element.20), channel_id=1, replica_groups=mesh['section'=16,'x'=4,'core'=2,'tp'=4] {'x','core','tp'}, dimensions={0} | all-to-all | bytes 1048576 | tf_op jit(solution)/shard_map/all_to_all | solution.py:241
  50.7 2.0 %shard_map.143 = bf16[32,64,128]{2,1,0:T(8,128)(2,1)S(1)} custom-call(bf16[32,64,128]{2,1,0:T(8,128)(2,1)S(1)} %all_to_all.48.rows_ref, f32[1,4096]{1,0:T(1,128)S(1)} %copy-done.1, bf16[432,4096]{1,0:T(8,128)(2,1)S(1)} %shard_map.141.near_ref, bf16[432,4096]{1,0:T(8,128)(2,1)S(1)} %collective-permute-done.far_ref), custom_call_target="tpu_custom_call" | custom-call | tf_op jit(solution)/shard_map/pallas_call | solution.py:225
  52.7 15.4 %all_to_all.49.parts_ref = bf16[32,64,128]{2,1,0:T(8,128)(2,1)S(1)} all-to-all(bf16[32,64,128]{2,1,0:T(8,128)(2,1)S(1)} %shard_map.143), channel_id=1, replica_groups=mesh['section'=16,'x'=4,'core'=2,'tp'=4] {'x','core','tp'}, dimensions={0} | all-to-all | bytes 1048576 | tf_op jit(solution)/shard_map/all_to_all | solution.py:241
  68.2 1.9 %collective-permute-start.1 = (bf16[128,128]{1,0:T(8,128)(2,1)S(1)}, bf16[128,128]{1,0:T(8,128)(2,1)S(1)}, u32[]{:S(2)}, u32[]{:S(2)}) collective-permute-start(bf16[128,128]{1,0:T(8,128)(2,1)S(1)} %shard_map.144), channel_id=1, source_target_pairs={{0,32},{32,64},{64,96},{96,128},{128,160},{160,192},{192,224},{224... | collective-permute-start | bytes 98312 | tf_op jit(solution)/shard_map/ppermute | solution.py:330
  70.1 8.6 %collective-permute-done.1.passed_ref = bf16[128,128]{1,0:T(8,128)(2,1)S(1)} collective-permute-done((bf16[128,128]{1,0:T(8,128)(2,1)S(1)}, bf16[128,128]{1,0:T(8,128)(2,1)S(1)}, u32[]{:S(2)}, u32[]{:S(2)}) %collective-permute-start.1) | collective-permute-done | bytes 32800 | tf_op jit(solution)/shard_map/ppermute | solution.py:330
  78.9 12.1 %all_to_all.50 = f32[32,1,128]{2,1,0:T(1,128)S(1)} all-to-all(f32[32,1,128]{2,1,0:T(1,128)S(1)} %bitcast.31), channel_id=1, replica_groups=mesh['section'=16,'x'=4,'core'=2,'tp'=4] {'x','core','tp'}, dimensions={0} | all-to-all | bytes 32768 | tf_op jit(solution)/shard_map/all_to_all | solution.py:241
  91.1 1.4 %shard_map.146 = (bf16[32,64,128]{2,1,0:T(8,128)(2,1)S(1)}, bf16[128,128]{1,0:T(8,128)(2,1)S(1)}, f32[128,128]{1,0:T(8,128)}, bf16[2,128,128]{2,1,0:T(8,128)(2,1)}) custom-call(f32[1,1]{1,0:T(1,128)S(6)} %copy.25.decay_ref, f32[32,128]{1,0:T(8,128)S(1)} %bitcast.29, bf16[8,128,128]{2,1,0:T(8,128)(2,1)S(1)} %get-tuple-element.24.prefix_in, ...), custom_call_target="tpu_custom_call" | custom-call | tf_op jit(solution)/shard_map/pallas_call | solution.py:225
  92.5 14.8 %all_to_all.51.rows_ref = bf16[32,64,128]{2,1,0:T(8,128)(2,1)S(1)} all-to-all(bf16[32,64,128]{2,1,0:T(8,128)(2,1)S(1)} %get-tuple-element.29), channel_id=1, replica_groups=mesh['section'=16,'x'=4,'core'=2,'tp'=4] {'x','core','tp'}, dimensions={0} | all-to-all | bytes 1048576 | tf_op jit(solution)/shard_map/all_to_all | solution.py:241
  107.3 2.0 %shard_map.147 = bf16[32,64,128]{2,1,0:T(8,128)(2,1)S(1)} custom-call(bf16[32,64,128]{2,1,0:T(8,128)(2,1)S(1)} %all_to_all.51.rows_ref, f32[1,4096]{1,0:T(1,128)S(1)} %copy-done.1, bf16[432,4096]{1,0:T(8,128)(2,1)S(1)} %shard_map.141.near_ref, bf16[432,4096]{1,0:T(8,128)(2,1)S(1)} %collective-permute-done.far_ref), custom_call_target="tpu_custom_call" | custom-call | tf_op jit(solution)/shard_map/pallas_call | solution.py:225
  109.3 15.4 %all_to_all.52.parts_ref = bf16[32,64,128]{2,1,0:T(8,128)(2,1)S(1)} all-to-all(bf16[32,64,128]{2,1,0:T(8,128)(2,1)S(1)} %shard_map.147), channel_id=1, replica_groups=mesh['section'=16,'x'=4,'core'=2,'tp'=4] {'x','core','tp'}, dimensions={0} | all-to-all | bytes 1048576 | tf_op jit(solution)/shard_map/all_to_all | solution.py:241
  124.7 1.9 %collective-permute-start.2 = (bf16[128,128]{1,0:T(8,128)(2,1)S(1)}, bf16[128,128]{1,0:T(8,128)(2,1)S(1)}, u32[]{:S(2)}, u32[]{:S(2)}) collective-permute-start(bf16[128,128]{1,0:T(8,128)(2,1)S(1)} %shard_map.148), channel_id=1, source_target_pairs={{0,32},{32,64},{64,96},{96,128},{128,160},{160,192},{192,224},{224... | collective-permute-start | bytes 98312 | tf_op jit(solution)/shard_map/ppermute | solution.py:330
  126.7 3.9 %collective-permute-done.2 = bf16[128,128]{1,0:T(8,128)(2,1)S(1)} collective-permute-done((bf16[128,128]{1,0:T(8,128)(2,1)S(1)}, bf16[128,128]{1,0:T(8,128)(2,1)S(1)}, u32[]{:S(2)}, u32[]{:S(2)}) %collective-permute-start.2) | collective-permute-done | bytes 32800 | tf_op jit(solution)/shard_map/ppermute | solution.py:330
  130.6 0.6 maximum_bitcast_fusion.1
  (11 shorter events, 0.4 us)
Async XLA Ops:
  0.6 0.8 copy-start
  2.2 17.3 %all-to-all-start = ((f32[32,1,128]{2,1,0:T(1,128)}), f32[32,1,128]{2,1,0:T(1,128)S(1)}, u32[]{:S(2)}, u32[]{:S(2)}) async-start(f32[32,1,128]{2,1,0:T(1,128)} %bitcast.5), calls=%async_computation | async-start | bytes 32768 | tf_op jit(solution)/shard_map/all_to_all | solution.py:241
  19.5 4.6 %copy-start.3 = (f32[32,1,128]{2,1,0:T(1,128)}, f32[32,1,128]{2,1,0:T(1,128)S(1)}, u32[]{:S(2)}) copy-start(f32[32,1,128]{2,1,0:T(1,128)S(1)} %all-to-all-done) | copy-start | bytes 49156
  19.5 11.2 %all-to-all-start.1 = ((bf16[8,128,128]{2,1,0:T(8,128)(2,1)}), bf16[8,128,128]{2,1,0:T(8,128)(2,1)}, u32[]{:S(2)}, u32[]{:S(2)}) async-start(bf16[8,128,128]{2,1,0:T(8,128)(2,1)} %maximum_bitcast_fusion), calls=%async_computation.1 | async-start | bytes 524288 | tf_op jit(solution)/shard_map/all_to_all | solution.py:241
  24.1 26.6 %copy-start.1 = (f32[1,4096]{1,0:T(1,128)S(1)}, f32[1,4096]{1,0:T(1,128)}, u32[]{:S(2)}) copy-start(f32[1,4096]{1,0:T(1,128)} %gain_ref.3) | copy-start | bytes 49156
  30.7 20.0 %collective-permute-start = (bf16[432,4096]{1,0:T(8,128)(2,1)S(1)}, bf16[432,4096]{1,0:T(8,128)(2,1)S(1)}, u32[]{:S(2)}, u32[]{:S(2)}) collective-permute-start(bf16[432,4096]{1,0:T(8,128)(2,1)S(1)} %shard_map.141.near_ref), channel_id=1, source_target_pairs={{0,4},{4,0},{1,5},{5,1},{2,6},{6,2},{3,7},{7,3},{8,12},{12,8},{9,1... | collective-permute-start | bytes 10616840 | tf_op jit(solution)/shard_map/ppermute | solution.py:237
  50.7 28.0 %copy-start.2 = (bf16[1,128,128]{2,1,0:T(8,128)(2,1)S(1)}, bf16[1,128,128]{2,1,0:T(8,128)(2,1)}, u32[]{:S(2)}) copy-start(bf16[1,128,128]{2,1,0:T(8,128)(2,1)} %param.14) | copy-start | bytes 98308
  68.2 10.5 %collective-permute-start.1 = (bf16[128,128]{1,0:T(8,128)(2,1)S(1)}, bf16[128,128]{1,0:T(8,128)(2,1)S(1)}, u32[]{:S(2)}, u32[]{:S(2)}) collective-permute-start(bf16[128,128]{1,0:T(8,128)(2,1)S(1)} %shard_map.144), channel_id=1, source_target_pairs={{0,32},{32,64},{64,96},{96,128},{128,160},{160,192},{192,224},{224... | collective-permute-start | bytes 98312 | tf_op jit(solution)/shard_map/ppermute | solution.py:330
  124.7 5.9 %collective-permute-start.2 = (bf16[128,128]{1,0:T(8,128)(2,1)S(1)}, bf16[128,128]{1,0:T(8,128)(2,1)S(1)}, u32[]{:S(2)}, u32[]{:S(2)}) collective-permute-start(bf16[128,128]{1,0:T(8,128)(2,1)S(1)} %shard_map.148), channel_id=1, source_target_pairs={{0,32},{32,64},{64,96},{96,128},{128,160},{160,192},{192,224},{224... | collective-permute-start | bytes 98312 | tf_op jit(solution)/shard_map/ppermute | solution.py:330

commit v3 on v2

--- a/solution.py
+++ b/solution.py
@@ -16,6 +16,7 @@
 BLOCKS = 32
 SHARDS = 8
 ROWS = 64
+TAIL = 16
 GROUPS = 3
 GROUP = UNITS // GROUPS
 EPS = 1e-6
@@ -43,8 +44,90 @@
     parts_ref[...] = jnp.concatenate([sums] * (BLOCKS // 8), axis=0)
 
 
-def first_squares_kernel(rows_ref, parts_ref):
-    write_square_sums(rows_ref[...], parts_ref)
+def started(pairs, sems):
+    copies = [pltpu.make_async_copy(*pair, sems.at[i]) for i, pair in enumerate(pairs)]
+    for copy in copies:
+        copy.start()
+    return copies
+
+
+def start_kernel(rows_hbm, keys_hbm, values_hbm, out_hbm, rows_ref, keys_ref, values_ref, out_ref, sems):
+    copies = started(
+        [(rows_hbm, rows_ref), (keys_hbm, keys_ref), (values_hbm, values_ref)], sems
+    )
+    copies[0].wait()
+    squares = rows_ref[...].astype(F32)
+    squares = squares * squares
+    sums = dot(jnp.ones((TAIL, HEAD), F32), squares, (1, 1), HIGH)
+    high = sums.astype(BF16).astype(F32)
+    middle = (sums - high).astype(BF16).astype(F32)
+    row = lax.broadcasted_iota(jnp.int32, (TAIL, HEAD), 0)
+    tail = jnp.where(row == 2, sums - high - middle, 0.0)
+    tail = jnp.where(row == 0, high, jnp.where(row == 1, middle, tail)).astype(BF16)
+    for index, ref in enumerate((keys_ref, values_ref)):
+        copies[1 + index].wait()
+        by_head = jnp.swapaxes(ref[...], 0, 1)
+        for shard in range(SHARDS):
+            out_ref[shard, index * ROWS : (index + 1) * ROWS] = by_head[shard]
+    for shard in range(SHARDS):
+        out_ref[shard, 2 * ROWS :] = tail
+    copy = pltpu.make_async_copy(out_ref, out_hbm, sems.at[3])
+    copy.start()
+    copy.wait()
+
+
+def merge_kernel(
+    decays_hbm,
+    lengths_hbm,
+    swapped_hbm,
+    rows_hbm,
+    memory_hbm,
+    gain_hbm,
+    key_gain_hbm,
+    linear_gain_hbm,
+    parts_ref,
+    prefix_ref,
+    rows_ref,
+    memory_ref,
+    consts_ref,
+    lengths_ref,
+    decays_ref,
+    tails_ref,
+    gains_ref,
+    sems,
+):
+    place = pl.ds(pl.multiple_of(block_place() * HEAD, HEAD), HEAD)
+    copies = started(
+        [
+            (swapped_hbm.at[:, pl.ds(2 * ROWS, TAIL)], tails_ref),
+            (lengths_hbm, lengths_ref),
+            (decays_hbm, decays_ref),
+            (gain_hbm.at[:, place], gains_ref.at[0]),
+            (key_gain_hbm.at[:, place], gains_ref.at[1]),
+            (linear_gain_hbm, gains_ref.at[2]),
+            (rows_hbm, rows_ref),
+            (memory_hbm, memory_ref),
+            (swapped_hbm.at[:, pl.ds(0, 2 * ROWS)], prefix_ref),
+        ],
+        sems,
+    )
+    copies[0].wait()
+    tails = tails_ref[0].astype(F32)
+    for shard in range(1, SHARDS):
+        tails = tails + tails_ref[shard].astype(F32)
+    sums = jnp.sum(tails, axis=0, keepdims=True) * (1.0 / 8)
+    for target in range(4):
+        parts_ref[target] = jnp.broadcast_to(sums, (8, HEAD))
+    for copy in copies[1:]:
+        copy.wait()
+    slot = lax.broadcasted_iota(jnp.int32, (1, SHARDS * ROWS), 1)
+    used = jnp.zeros((1, SHARDS * ROWS), jnp.int32)
+    for shard in range(SHARDS):
+        used = jnp.where(slot // ROWS == shard, lengths_ref[0, shard], used)
+    consts_ref[0:1] = jnp.where(slot % ROWS < used, 0.0, MASKED)
+    for index in range(3):
+        consts_ref[1:2, index * HEAD : (index + 1) * HEAD] = gains_ref[index]
+    consts_ref[1:2, 3 * HEAD :] = decays_ref[0:1]
 
 
 def later_squares_kernel(passed_ref, entering_ref, rows_ref, parts_ref):
@@ -53,45 +136,17 @@
     write_square_sums(rows, parts_ref)
 
 
-def attention_kernel(tick, decay_ref, parts_in, prefix_in, rows_in, memory_in, *refs):
+def attention_kernel(
+    tick, parts_ref, consts_ref, prefix_ref, rows_ref, memory_ref, *refs
+):
     scale = HEAD**-0.5
-    place = pl.ds(pl.multiple_of(block_place() * HEAD, HEAD), HEAD)
-    if tick == 0:
-        lengths_hbm, gain_hbm, key_gain_hbm, linear_gain_hbm = refs[:4]
-        spread_ref, mixed_ref, new_memory_ref, turn_ref, consts_ref, prefix_ref = refs[4:10]
-        lengths_ref, gains_ref, parts_ref, rows_ref, memory_ref, sems = refs[10:]
-        copies = [
-            (parts_in, parts_ref),
-            (rows_in, rows_ref),
-            (gain_hbm.at[:, place], gains_ref.at[0]),
-            (key_gain_hbm.at[:, place], gains_ref.at[1]),
-            (linear_gain_hbm, gains_ref.at[2]),
-            (memory_in, memory_ref),
-            (lengths_hbm, lengths_ref),
-            (prefix_in, prefix_ref),
-        ]
-        copies = [pltpu.make_async_copy(*pair, sems.at[i]) for i, pair in enumerate(copies)]
-        for copy in copies:
-            copy.start()
-        for copy in copies[:-1]:
-            copy.wait()
-        slot = lax.broadcasted_iota(jnp.int32, (1, SHARDS * ROWS), 1)
-        used = jnp.zeros((1, SHARDS * ROWS), jnp.int32)
-        for shard in range(SHARDS):
-            used = jnp.where(slot // ROWS == shard, lengths_ref[0, shard], used)
-        barred = jnp.where(slot % ROWS < used, 0.0, MASKED)
-        consts_ref[0:1] = barred
-        gain, key_gain, linear_gain = [gains_ref[index] for index in range(3)]
-        for index in range(3):
-            consts_ref[1:2, index * HEAD : (index + 1) * HEAD] = gains_ref[index]
-    else:
-        past_ref, consts_ref, spread_ref, mixed_ref, new_memory_ref, turn_ref = refs
-        parts_ref, prefix_ref, rows_ref, memory_ref = parts_in, prefix_in, rows_in, memory_in
-        barred = consts_ref[0:1]
-        gain, key_gain, linear_gain = [
-            consts_ref[1:2, index * HEAD : (index + 1) * HEAD] for index in range(3)
-        ]
-    decay = decay_ref[0, 0]
+    if tick:
+        past_ref, *refs = refs
+    spread_ref, mixed_ref, new_memory_ref, turn_ref = refs
+    barred = consts_ref[0:1]
+    gain, key_gain, linear_gain, decay = [
+        consts_ref[1:2, index * HEAD : (index + 1) * HEAD] for index in range(4)
+    ]
     sums = dot(parts_ref[...], jnp.ones((BLOCKS, HEAD), F32), (0, 0), HIGH)
     rows = rows_ref[...].astype(F32)
     normed = rows * lax.rsqrt(sums * (1.0 / DIM) + EPS) * gain
@@ -114,14 +169,12 @@
         -decay * (row + 1.0)
     )
     tail = keys.astype(F32) * jnp.exp(-decay * (TOK - 1.0 - row))
-    new_memory_ref[...] = memory * jnp.exp(jnp.full(shape, -decay * TOK, F32)) + (
+    new_memory_ref[...] = memory * jnp.exp(-decay * TOK) + (
         dot(tail, wide, (0, 0), HIGH) * scale
     )
     spread = jnp.mean(raw * raw, axis=1, keepdims=True)
     linear = raw * lax.rsqrt(spread + EPS) * linear_gain
 
-    if tick == 0:
-        copies[-1].wait()
     prefix_keys = prefix_ref[:, :ROWS, :].reshape(SHARDS * ROWS, HEAD)
     prefix_values = prefix_ref[:, ROWS:, :].reshape(SHARDS * ROWS, HEAD)
     prefix_scores = dot(queries, prefix_keys, (1, 1)) * scale + barred
@@ -179,15 +232,14 @@
             out_ref[first // HEAD + block] = down[:, block * HEAD : (block + 1) * HEAD].astype(BF16)
 
 
-def prepare_kernel(gate_up_hbm, down_hbm, weights_ref, raw_ref, sems):
-    copies = []
+def prepare_kernel(decay_ref, gate_up_hbm, down_hbm, weights_ref, decays_ref, raw_ref, sems):
+    decays_ref[...] = jnp.full((8, HEAD), decay_ref[0, 0], F32)
+    pairs = []
     for group in range(GROUPS):
         span = pl.ds(group * GROUP, GROUP)
-        copies.append((gate_up_hbm.at[span], raw_ref.at[span]))
-    copies.append((down_hbm, weights_ref.at[pl.ds(2 * UNITS, UNITS)]))
-    copies = [pltpu.make_async_copy(*pair, sems.at[i]) for i, pair in enumerate(copies)]
-    for copy in copies:
-        copy.start()
+        pairs.append((gate_up_hbm.at[span], raw_ref.at[span]))
+    pairs.append((down_hbm, weights_ref.at[pl.ds(2 * UNITS, UNITS)]))
+    copies = started(pairs, sems)
     for group in range(GROUPS):
         copies[group].wait()
 
@@ -202,19 +254,19 @@
 
 def finish_kernel(parts_ref, mixed_ref, out_ref):
     for half in range(2):
-        total = jnp.zeros((HALF, HEAD), F32)
+        place = slice(half * HALF, (half + 1) * HALF)
+        total = mixed_ref[place].astype(F32)
         for block in range(BLOCKS):
             if block // 4 % 2 == half:
                 total = total + parts_ref[block].astype(F32)
-        place = slice(half * HALF, (half + 1) * HALF)
-        out_ref[place] = (mixed_ref[place].astype(F32) + total).astype(BF16)
+        out_ref[place] = total.astype(BF16)
 
 
 def shape_of(*shape, dtype=BF16):
     return jax.ShapeDtypeStruct(shape, dtype)
 
 
-def local_call(kernel, outs, ins, scratch=(), spaces=None, cost=None, mib=8):
+def local_call(kernel, outs, ins, scratch=(), spaces=None, out_space=pltpu.VMEM, cost=None, mib=8):
     spaces = spaces or {}
     ins = [
         pltpu.with_memory_space_constraint(value, spaces[i])
@@ -226,7 +278,7 @@
         kernel,
         out_shape=outs,
         in_specs=[pl.BlockSpec(memory_space=spaces.get(i, pltpu.VMEM)) for i in range(len(ins))],
-        out_specs=jax.tree.map(lambda _: pl.BlockSpec(memory_space=pltpu.VMEM), outs),
+        out_specs=jax.tree.map(lambda _: pl.BlockSpec(memory_space=out_space), outs),
         scratch_shapes=list(scratch),
         compiler_params=pltpu.CompilerParams(vmem_limit_bytes=mib << 20),
         cost_estimate=cost,
@@ -257,64 +309,84 @@
     lengths,
 ):
     rows = arriving[0]
-    parts = local_call(first_squares_kernel, shape_of(BLOCKS, HEAD, dtype=F32), (rows,))
-    weights = local_call(
+    sent = local_call(
+        start_kernel,
+        shape_of(SHARDS, 2 * ROWS + TAIL, HEAD),
+        (rows, prefix_keys[0], prefix_values[0]),
+        scratch=(
+            pltpu.VMEM((TOK, HEAD), BF16),
+            pltpu.VMEM((ROWS, SHARDS, HEAD), BF16),
+            pltpu.VMEM((ROWS, SHARDS, HEAD), BF16),
+            pltpu.VMEM((SHARDS, 2 * ROWS + TAIL, HEAD), BF16),
+            pltpu.SemaphoreType.DMA((4,)),
+        ),
+        spaces=dict.fromkeys(range(3), pltpu.HBM),
+        out_space=pltpu.HBM,
+    )
+    sent = exchanged(sent, ("x", "core"))
+    weights, decays = local_call(
         prepare_kernel,
-        shape_of(3 * UNITS, DIM),
-        (gate_up[0], down_weight[0]),
+        (shape_of(3 * UNITS, DIM), shape_of(8, HEAD, dtype=F32)),
+        (decay_rate, gate_up[0], down_weight[0]),
         scratch=(pltpu.VMEM((UNITS, 2, DIM), BF16), pltpu.SemaphoreType.DMA((GROUPS + 1,))),
-        spaces=dict.fromkeys(range(2), pltpu.HBM),
+        spaces={0: pltpu.SMEM, 1: pltpu.HBM, 2: pltpu.HBM},
         cost=pl.CostEstimate(flops=0, bytes_accessed=8 << 20, transcendentals=0),
         mib=16,
     )
-    prefix = jnp.concatenate([prefix_keys[0], prefix_values[0]], axis=0)
-    prefix = jnp.transpose(prefix, (1, 0, 2))
-    parts = exchanged(parts)
-    prefix, parts = lax.optimization_barrier((prefix, parts))
-    prefix = exchanged(prefix, ("x", "core"))
-    prefix, sent_weights = lax.optimization_barrier((prefix, weights))
+    parts, prefix, rows, memory, consts = local_call(
+        merge_kernel,
+        (
+            shape_of(4, 8, HEAD, dtype=F32),
+            shape_of(SHARDS, 2 * ROWS, HEAD),
+            shape_of(TOK, HEAD),
+            shape_of(HEAD, HEAD, dtype=F32),
+            shape_of(8, SHARDS * ROWS, dtype=F32),
+        ),
+        (
+            decays,
+            lengths,
+            sent,
+            rows,
+            state_in[0, 0],
+            gain_attention,
+            gain_key,
+            gain_linear,
+        ),
+        scratch=(
+            pltpu.SMEM((1, SHARDS), jnp.int32),
+            pltpu.VMEM((8, HEAD), F32),
+            pltpu.VMEM((SHARDS, TAIL, HEAD), BF16),
+            pltpu.VMEM((3, 1, HEAD), F32),
+            pltpu.SemaphoreType.DMA((9,)),
+        ),
+        spaces=dict.fromkeys(range(8), pltpu.HBM),
+    )
+    parts, sent_weights = lax.optimization_barrier((parts, weights))
     far_weights = swapped(sent_weights)
-    memory = state_in[0, 0]
+    parts = exchanged(parts, "tp").reshape(BLOCKS, HEAD)
+    size = lax.axis_size("section")
+    onward = [(i, (i + 1) % size) for i in range(size)]
+    past = ()
     arrived = []
     for tick in range(TICKS):
         if tick:
             rows, parts = local_call(
                 later_squares_kernel,
                 (shape_of(TOK, HEAD), shape_of(BLOCKS, HEAD, dtype=F32)),
-                (arrived[-1], entering[tick - 1]),
+                (passed, entering[tick - 1]),
             )
             parts = exchanged(parts)
-        outs = (
-            shape_of(BLOCKS, HALF, HEAD),
-            shape_of(TOK, HEAD),
-            shape_of(HEAD, HEAD, dtype=F32),
-            shape_of(2, TOK, HEAD),
+        spread, mixed, memory, turn = local_call(
+            functools.partial(attention_kernel, tick),
+            (
+                shape_of(BLOCKS, HALF, HEAD),
+                shape_of(TOK, HEAD),
+                shape_of(HEAD, HEAD, dtype=F32),
+                shape_of(2, TOK, HEAD),
+            ),
+            (parts, consts, prefix, rows, memory, *past),
         )
-        ins = (decay_rate, parts, prefix, rows, memory)
-        kernel = functools.partial(attention_kernel, tick)
-        if tick == 0:
-            spread, mixed, memory, turn, consts, prefix = local_call(
-                kernel,
-                (
-                    *outs,
-                    shape_of(8, SHARDS * ROWS, dtype=F32),
-                    shape_of(SHARDS, 2 * ROWS, HEAD),
-                ),
-                (*ins, lengths, gain_attention, gain_key, gain_linear),
-                scratch=(
-                    pltpu.SMEM((1, SHARDS), jnp.int32),
-                    pltpu.VMEM((3, 1, HEAD), F32),
-                    pltpu.VMEM((BLOCKS, HEAD), F32),
-                    pltpu.VMEM((TOK, HEAD), BF16),
-                    pltpu.VMEM((HEAD, HEAD), F32),
-                    pltpu.SemaphoreType.DMA((8,)),
-                ),
-                spaces={0: pltpu.SMEM, **dict.fromkeys(range(1, 9), pltpu.HBM)},
-            )
-        else:
-            spread, mixed, memory, turn = local_call(
-                kernel, outs, (*ins, turn, consts), spaces={0: pltpu.SMEM}
-            )
+        past = (turn,)
         spread = exchanged(spread)
         down = local_call(
             feed_kernel,
@@ -325,10 +397,8 @@
         )
         down = exchanged(down)
         finished = local_call(finish_kernel, shape_of(TOK, HEAD), (down, mixed))
-        size = lax.axis_size("section")
-        arrived.append(
-            lax.ppermute(finished, "section", [(i, (i + 1) % size) for i in range(size)])
-        )
+        passed = lax.ppermute(finished, "section", onward)
+        arrived.append(passed)
     return (jnp.stack(arrived)[:, None], memory[None, None])
 
 

time: 132 us -> 127 us (0.962)
  blocking collectives: 71.8 us -> 79.4 us
  waiting for transfers between devices: 22.3 us -> 15 us
  starting transfers between devices: 21.7 us -> 17.7 us
    all_to_all x5 -> x6, blocking collectives: 71.8 us -> 79.4 us  [exchanged(): return lax.all_to_all(value, axes, 0, 0, tiled=True)]
    all_to_all x2 -> x1, waiting for transfers between devices: 9.78 us -> 3.66 us  [exchanged(): return lax.all_to_all(value, axes, 0, 0, tiled=True)]
    all_to_all x2 -> x1, starting transfers between devices: 15 us -> 10.8 us  [exchanged(): return lax.all_to_all(value, axes, 0, 0, tiled=True)]
    pallas_call x9 -> x10, Pallas kernels: 10.9 us -> 11.8 us  [local_call(): pl.pallas_call(kernel, out_shape=outs, in_specs=[pl.BlockSpec(memory_spac...]
  transfers between devices with their start and end apart: 5 -> 4, of which waited for: 4 -> 3; matrix products, arithmetic and copies ran while one was open for 1% -> 0% of each run, Pallas kernels for 3% -> 2%
where the time goes in v3:
time: 127 us; the launch traced here: 126 us
  blocking collectives  79.4 us (63%)
  starting transfers between devices  17.7 us (14%)
  waiting for transfers between devices  15 us (12%)
  Pallas kernels  11.8 us (9%)
  between operations  1.38 us (1%)
    all_to_all x6, blocking collectives, exchanged(): return lax.all_to_all(value, axes, 0, 0, tiled=True)  79.4 us
    pallas_call x10, Pallas kernels, local_call(): pl.pallas_call(kernel, out_shape=outs, in_specs=[pl.BlockSpec(memory_spac...  11.8 us
    ppermute x2, waiting for transfers between devices, per_device(): passed = lax.ppermute(finished, 'section', onward)  11.3 us
    all_to_all x1, starting transfers between devices, exchanged(): return lax.all_to_all(value, axes, 0, 0, tiled=True)  10.8 us
    ppermute x2, starting transfers between devices, per_device(): passed = lax.ppermute(finished, 'section', onward)  3.84 us
    all_to_all x1, waiting for transfers between devices, exchanged(): return lax.all_to_all(value, axes, 0, 0, tiled=True)  3.66 us
    ppermute x1, starting transfers between devices, swapped(): return lax.ppermute(value, 'core', [(0, 1), (1, 0)])  2.99 us
  transfers between devices with their start and end apart: 4, of which 3 were waited for; matrix products, arithmetic and copies ran while one was open for 0% of the time, Pallas kernels for 2%

profile of v3, /device:TPU:1, one launch (start us, length us, event | category | flops | bytes accessed | tf_op | source)
XLA Modules:
  0.0 126.4 jit_solution(18155549394174690461)
XLA Ops:
  0.6 1.8 %shard_map.141 = bf16[8,144,128]{2,1,0:T(8,128)(2,1)} custom-call(bf16[128,128]{1,0:T(8,128)(2,1)} %bitcast.28, bf16[64,8,128]{2,1,0:T(8,128)(2,1)} %bitcast.26, bf16[64,8,128]{2,1,0:T(8,128)(2,1)} %bitcast.27), custom_call_target="tpu_custom_call" | custom-call | tf_op jit(solution)/shard_map/pallas_call | solution.py:277
  2.5 10.8 %all-to-all-start = ((bf16[8,144,128]{2,1,0:T(8,128)(2,1)}), bf16[8,144,128]{2,1,0:T(8,128)(2,1)}, u32[]{:S(2)}, u32[]{:S(2)}) async-start(bf16[8,144,128]{2,1,0:T(8,128)(2,1)} %shard_map.141), calls=%async_computation | async-start | bytes 589824 | tf_op jit(solution)/shard_map/all_to_all | solution.py:293
  13.9 2.0 %shard_map.140 = (bf16[432,4096]{1,0:T(8,128)(2,1)S(1)}, f32[8,128]{1,0:T(8,128)S(1)}) custom-call(f32[1,1]{1,0:T(1,128)S(6)} %copy.18.decay_ref, bf16[144,2,4096]{2,1,0:T(2,128)(2,1)} %bitcast.24, bf16[144,4096]{1,0:T(8,128)(2,1)} %bitcast.25), custom_call_target="tpu_custom_call" | custom-call | bytes 8388608 | tf_op jit(solution)/shard_map/pallas_call | solution.py:277
  16.0 0.6 copy-done.2
  16.6 3.7 %all-to-all-done.swapped_hbm = bf16[8,144,128]{2,1,0:T(8,128)(2,1)} async-done(((bf16[8,144,128]{2,1,0:T(8,128)(2,1)}), bf16[8,144,128]{2,1,0:T(8,128)(2,1)}, u32[]{:S(2)}, u32[]{:S(2)}) %all-to-all-start) | async-done | bytes 294944 | tf_op jit(solution)/shard_map/all_to_all | solution.py:293
  20.2 1.2 shard_map.142
  21.4 3.0 %collective-permute-start = (bf16[432,4096]{1,0:T(8,128)(2,1)S(1)}, bf16[432,4096]{1,0:T(8,128)(2,1)S(1)}, u32[]{:S(2)}, u32[]{:S(2)}) collective-permute-start(bf16[432,4096]{1,0:T(8,128)(2,1)S(1)} %get-tuple-element.29.near_ref), channel_id=1, source_target_pairs={{0,4},{4,0},{1,5},{5,1},{2,6},{6,2},{3,7},{7,3},{8,12},{12,8},{9,1... | collective-permute-start | bytes 10616840 | tf_op jit(solution)/shard_map/ppermute | solution.py:289
  24.4 6.6 %all_to_all.41 = f32[4,8,128]{2,1,0:T(8,128)S(1)} all-to-all(f32[4,8,128]{2,1,0:T(8,128)S(1)} %get-tuple-element.23), channel_id=1, replica_groups=mesh['section'=16,'x'=4,'core'=2,'tp'=4] {'tp'}, dimensions={0} | all-to-all | bytes 32768 | tf_op jit(solution)/shard_map/all_to_all | solution.py:293
  31.0 0.9 shard_map.143
  31.9 15.2 %all_to_all.42.rows_ref = bf16[32,64,128]{2,1,0:T(8,128)(2,1)S(1)} all-to-all(bf16[32,64,128]{2,1,0:T(8,128)(2,1)S(1)} %get-tuple-element.28), channel_id=1, replica_groups=mesh['section'=16,'x'=4,'core'=2,'tp'=4] {'x','core','tp'}, dimensions={0} | all-to-all | bytes 1048576 | tf_op jit(solution)/shard_map/all_to_all | solution.py:293
  47.1 2.0 %shard_map.144 = bf16[32,64,128]{2,1,0:T(8,128)(2,1)S(1)} custom-call(bf16[32,64,128]{2,1,0:T(8,128)(2,1)S(1)} %all_to_all.42.rows_ref, f32[1,4096]{1,0:T(1,128)S(1)} %copy-done, bf16[432,4096]{1,0:T(8,128)(2,1)S(1)} %get-tuple-element.29.near_ref, bf16[432,4096]{1,0:T(8,128)(2,1)S(1)} %collective-permute-done.far_ref), custom_call_target="tpu_custom_call" | custom-call | tf_op jit(solution)/shard_map/pallas_call | solution.py:277
  49.1 15.4 %all_to_all.43.parts_ref = bf16[32,64,128]{2,1,0:T(8,128)(2,1)S(1)} all-to-all(bf16[32,64,128]{2,1,0:T(8,128)(2,1)S(1)} %shard_map.144), channel_id=1, replica_groups=mesh['section'=16,'x'=4,'core'=2,'tp'=4] {'x','core','tp'}, dimensions={0} | all-to-all | bytes 1048576 | tf_op jit(solution)/shard_map/all_to_all | solution.py:293
  64.5 0.1 shard_map.145
  64.6 1.9 %collective-permute-start.1 = (bf16[128,128]{1,0:T(8,128)(2,1)S(1)}, bf16[128,128]{1,0:T(8,128)(2,1)S(1)}, u32[]{:S(2)}, u32[]{:S(2)}) collective-permute-start(bf16[128,128]{1,0:T(8,128)(2,1)S(1)} %shard_map.145), channel_id=1, source_target_pairs={{0,32},{32,64},{64,96},{96,128},{128,160},{160,192},{192,224},{224... | collective-permute-start | bytes 98312 | tf_op jit(solution)/shard_map/ppermute | solution.py:400
  66.5 7.4 %collective-permute-done.1.passed_ref = bf16[128,128]{1,0:T(8,128)(2,1)S(1)} collective-permute-done((bf16[128,128]{1,0:T(8,128)(2,1)S(1)}, bf16[128,128]{1,0:T(8,128)(2,1)S(1)}, u32[]{:S(2)}, u32[]{:S(2)}) %collective-permute-start.1) | collective-permute-done | bytes 32800 | tf_op jit(solution)/shard_map/ppermute | solution.py:400
  73.9 0.2 shard_map.146
  74.1 12.1 %all_to_all.44 = f32[32,1,128]{2,1,0:T(1,128)S(1)} all-to-all(f32[32,1,128]{2,1,0:T(1,128)S(1)} %bitcast.23), channel_id=1, replica_groups=mesh['section'=16,'x'=4,'core'=2,'tp'=4] {'x','core','tp'}, dimensions={0} | all-to-all | bytes 32768 | tf_op jit(solution)/shard_map/all_to_all | solution.py:293
  86.2 1.4 %shard_map.147 = (bf16[32,64,128]{2,1,0:T(8,128)(2,1)S(1)}, bf16[128,128]{1,0:T(8,128)(2,1)S(1)}, f32[128,128]{1,0:T(8,128)}, bf16[2,128,128]{2,1,0:T(8,128)(2,1)}) custom-call(f32[32,128]{1,0:T(8,128)S(1)} %bitcast.20, f32[8,512]{1,0:T(8,128)S(1)} %get-tuple-element.24.consts_ref, bf16[8,128,128]{2,1,0:T(8,128)(2,1)S(1)} %get-tuple-element.25.prefix_ref, ...), custom_call_target="tpu_custom_call" | custom-call | tf_op jit(solution)/shard_map/pallas_call | solution.py:277
  87.6 14.8 %all_to_all.45.rows_ref = bf16[32,64,128]{2,1,0:T(8,128)(2,1)S(1)} all-to-all(bf16[32,64,128]{2,1,0:T(8,128)(2,1)S(1)} %get-tuple-element.35), channel_id=1, replica_groups=mesh['section'=16,'x'=4,'core'=2,'tp'=4] {'x','core','tp'}, dimensions={0} | all-to-all | bytes 1048576 | tf_op jit(solution)/shard_map/all_to_all | solution.py:293
  102.4 2.0 %shard_map.148 = bf16[32,64,128]{2,1,0:T(8,128)(2,1)S(1)} custom-call(bf16[32,64,128]{2,1,0:T(8,128)(2,1)S(1)} %all_to_all.45.rows_ref, f32[1,4096]{1,0:T(1,128)S(1)} %copy-done, bf16[432,4096]{1,0:T(8,128)(2,1)S(1)} %get-tuple-element.29.near_ref, bf16[432,4096]{1,0:T(8,128)(2,1)S(1)} %collective-permute-done.far_ref), custom_call_target="tpu_custom_call" | custom-call | tf_op jit(solution)/shard_map/pallas_call | solution.py:277
  104.5 15.4 %all_to_all.46.parts_ref = bf16[32,64,128]{2,1,0:T(8,128)(2,1)S(1)} all-to-all(bf16[32,64,128]{2,1,0:T(8,128)(2,1)S(1)} %shard_map.148), channel_id=1, replica_groups=mesh['section'=16,'x'=4,'core'=2,'tp'=4] {'x','core','tp'}, dimensions={0} | all-to-all | bytes 1048576 | tf_op jit(solution)/shard_map/all_to_all | solution.py:293
  119.9 1.9 %collective-permute-start.2 = (bf16[128,128]{1,0:T(8,128)(2,1)S(1)}, bf16[128,128]{1,0:T(8,128)(2,1)S(1)}, u32[]{:S(2)}, u32[]{:S(2)}) collective-permute-start(bf16[128,128]{1,0:T(8,128)(2,1)S(1)} %shard_map.149), channel_id=1, source_target_pairs={{0,32},{32,64},{64,96},{96,128},{128,160},{160,192},{192,224},{224... | collective-permute-start | bytes 98312 | tf_op jit(solution)/shard_map/ppermute | solution.py:400
  121.8 3.9 %collective-permute-done.2 = bf16[128,128]{1,0:T(8,128)(2,1)S(1)} collective-permute-done((bf16[128,128]{1,0:T(8,128)(2,1)S(1)}, bf16[128,128]{1,0:T(8,128)(2,1)S(1)}, u32[]{:S(2)}, u32[]{:S(2)}) %collective-permute-start.2) | collective-permute-done | bytes 32800 | tf_op jit(solution)/shard_map/ppermute | solution.py:400
  125.8 0.6 maximum_bitcast_fusion
  (7 shorter events, 0.1 us)
Async XLA Ops:
  0.6 46.5 %copy-start = (f32[1,4096]{1,0:T(1,128)S(1)}, f32[1,4096]{1,0:T(1,128)}, u32[]{:S(2)}) copy-start(f32[1,4096]{1,0:T(1,128)} %gain_ref.3) | copy-start | bytes 49156
  2.5 17.8 %all-to-all-start = ((bf16[8,144,128]{2,1,0:T(8,128)(2,1)}), bf16[8,144,128]{2,1,0:T(8,128)(2,1)}, u32[]{:S(2)}, u32[]{:S(2)}) async-start(bf16[8,144,128]{2,1,0:T(8,128)(2,1)} %shard_map.141), calls=%async_computation | async-start | bytes 589824 | tf_op jit(solution)/shard_map/all_to_all | solution.py:293
  16.0 0.6 copy-start.2
  21.4 25.7 %collective-permute-start = (bf16[432,4096]{1,0:T(8,128)(2,1)S(1)}, bf16[432,4096]{1,0:T(8,128)(2,1)S(1)}, u32[]{:S(2)}, u32[]{:S(2)}) collective-permute-start(bf16[432,4096]{1,0:T(8,128)(2,1)S(1)} %get-tuple-element.29.near_ref), channel_id=1, source_target_pairs={{0,4},{4,0},{1,5},{5,1},{2,6},{6,2},{3,7},{7,3},{8,12},{12,8},{9,1... | collective-permute-start | bytes 10616840 | tf_op jit(solution)/shard_map/ppermute | solution.py:289
  47.1 26.8 %copy-start.1 = (bf16[1,128,128]{2,1,0:T(8,128)(2,1)S(1)}, bf16[1,128,128]{2,1,0:T(8,128)(2,1)}, u32[]{:S(2)}) copy-start(bf16[1,128,128]{2,1,0:T(8,128)(2,1)} %param.14) | copy-start | bytes 98308
  64.6 9.3 %collective-permute-start.1 = (bf16[128,128]{1,0:T(8,128)(2,1)S(1)}, bf16[128,128]{1,0:T(8,128)(2,1)S(1)}, u32[]{:S(2)}, u32[]{:S(2)}) collective-permute-start(bf16[128,128]{1,0:T(8,128)(2,1)S(1)} %shard_map.145), channel_id=1, source_target_pairs={{0,32},{32,64},{64,96},{96,128},{128,160},{160,192},{192,224},{224... | collective-permute-start | bytes 98312 | tf_op jit(solution)/shard_map/ppermute | solution.py:400
  119.9 5.9 %collective-permute-start.2 = (bf16[128,128]{1,0:T(8,128)(2,1)S(1)}, bf16[128,128]{1,0:T(8,128)(2,1)S(1)}, u32[]{:S(2)}, u32[]{:S(2)}) collective-permute-start(bf16[128,128]{1,0:T(8,128)(2,1)S(1)} %shard_map.149), channel_id=1, source_target_pairs={{0,32},{32,64},{64,96},{96,128},{128,160},{160,192},{192,224},{224... | collective-permute-start | bytes 98312 | tf_op jit(solution)/shard_map/ppermute | solution.py:400

commit v4 on v3

--- a/solution.py
+++ b/solution.py
@@ -67,13 +67,18 @@
     for index, ref in enumerate((keys_ref, values_ref)):
         copies[1 + index].wait()
         by_head = jnp.swapaxes(ref[...], 0, 1)
+        span = pl.ds(index * ROWS, ROWS)
         for shard in range(SHARDS):
-            out_ref[shard, index * ROWS : (index + 1) * ROWS] = by_head[shard]
-    for shard in range(SHARDS):
-        out_ref[shard, 2 * ROWS :] = tail
-    copy = pltpu.make_async_copy(out_ref, out_hbm, sems.at[3])
-    copy.start()
-    copy.wait()
+            out_ref[shard, span] = by_head[shard]
+            if index:
+                out_ref[shard, 2 * ROWS :] = tail
+        span = pl.ds(index * ROWS, ROWS + index * TAIL)
+        copies.append(
+            pltpu.make_async_copy(out_ref.at[:, span], out_hbm.at[:, span], sems.at[3 + index])
+        )
+        copies[-1].start()
+    for copy in copies[3:]:
+        copy.wait()
 
 
 def merge_kernel(
@@ -136,13 +141,21 @@
     write_square_sums(rows, parts_ref)
 
 
+def memory_kernel(consts_ref, memory_ref, turn_ref, out_ref):
+    decay = consts_ref[1:2, 3 * HEAD :]
+    row = lax.broadcasted_iota(jnp.int32, (TOK, HEAD), 0).astype(F32)
+    tail = turn_ref[0].astype(F32) * jnp.exp(-decay * (TOK - 1.0 - row))
+    update = dot(tail, turn_ref[1].astype(F32), (0, 0), HIGH) * HEAD**-0.5
+    out_ref[...] = memory_ref[...] * jnp.exp(-decay * TOK) + update
+
+
 def attention_kernel(
     tick, parts_ref, consts_ref, prefix_ref, rows_ref, memory_ref, *refs
 ):
     scale = HEAD**-0.5
     if tick:
         past_ref, *refs = refs
-    spread_ref, mixed_ref, new_memory_ref, turn_ref = refs
+    spread_ref, mixed_ref, turn_ref = refs[:3]
     barred = consts_ref[0:1]
     gain, key_gain, linear_gain, decay = [
         consts_ref[1:2, index * HEAD : (index + 1) * HEAD] for index in range(4)
@@ -154,6 +167,8 @@
     keys = (normed * key_gain).astype(BF16)
     turn_ref[0] = keys
     turn_ref[1] = queries
+    if tick == 0:
+        memory_kernel(consts_ref, memory_ref, turn_ref, refs[3])
 
     shape = (TOK, TOK)
     row = lax.broadcasted_iota(jnp.int32, shape, 0)
@@ -167,10 +182,6 @@
     wide = queries.astype(F32)
     raw = dot(weights, queries, (1, 0)) + dot(wide, memory, (1, 0), HIGH) * jnp.exp(
         -decay * (row + 1.0)
-    )
-    tail = keys.astype(F32) * jnp.exp(-decay * (TOK - 1.0 - row))
-    new_memory_ref[...] = memory * jnp.exp(-decay * TOK) + (
-        dot(tail, wide, (0, 0), HIGH) * scale
     )
     spread = jnp.mean(raw * raw, axis=1, keepdims=True)
     linear = raw * lax.rsqrt(spread + EPS) * linear_gain
@@ -318,7 +329,7 @@
             pltpu.VMEM((ROWS, SHARDS, HEAD), BF16),
             pltpu.VMEM((ROWS, SHARDS, HEAD), BF16),
             pltpu.VMEM((SHARDS, 2 * ROWS + TAIL, HEAD), BF16),
-            pltpu.SemaphoreType.DMA((4,)),
+            pltpu.SemaphoreType.DMA((5,)),
         ),
         spaces=dict.fromkeys(range(3), pltpu.HBM),
         out_space=pltpu.HBM,
@@ -376,16 +387,15 @@
                 (passed, entering[tick - 1]),
             )
             parts = exchanged(parts)
-        spread, mixed, memory, turn = local_call(
-            functools.partial(attention_kernel, tick),
-            (
-                shape_of(BLOCKS, HALF, HEAD),
-                shape_of(TOK, HEAD),
-                shape_of(HEAD, HEAD, dtype=F32),
-                shape_of(2, TOK, HEAD),
-            ),
-            (parts, consts, prefix, rows, memory, *past),
-        )
+        outs = (shape_of(BLOCKS, HALF, HEAD), shape_of(TOK, HEAD), shape_of(2, TOK, HEAD))
+        state = shape_of(HEAD, HEAD, dtype=F32)
+        kernel = functools.partial(attention_kernel, tick)
+        ins = (parts, consts, prefix, rows, memory, *past)
+        if tick == 0:
+            spread, mixed, turn, memory = local_call(kernel, (*outs, state), ins)
+        else:
+            spread, mixed, turn = local_call(kernel, outs, ins)
+            memory = local_call(memory_kernel, state, (consts, memory, turn))
         past = (turn,)
         spread = exchanged(spread)
         down = local_call(

time: 127 us -> 127 us (level)
    pallas_call x10 -> x11, Pallas kernels: 11.8 us -> 12.2 us  [local_call(): pl.pallas_call(kernel, out_shape=outs, in_specs=[pl.BlockSpec(memory_spac...]
  transfers between devices with their start and end apart: 4 -> 4, of which waited for: 3 -> 3; matrix products, arithmetic and copies ran while one was open for 0% -> 0% of each run, Pallas kernels for 2% -> 3%
where the time goes in v4:
time: 127 us; the launch traced here: 126 us
  blocking collectives  79.4 us (63%)
  starting transfers between devices  17.7 us (14%)
  waiting for transfers between devices  14.1 us (11%)
  Pallas kernels  12.2 us (10%)
  between operations  1.39 us (1%)
    all_to_all x6, blocking collectives, exchanged(): return lax.all_to_all(value, axes, 0, 0, tiled=True)  79.4 us
    pallas_call x11, Pallas kernels, local_call(): pl.pallas_call(kernel, out_shape=outs, in_specs=[pl.BlockSpec(memory_spac...  12.2 us
    all_to_all x1, starting transfers between devices, exchanged(): return lax.all_to_all(value, axes, 0, 0, tiled=True)  10.8 us
    ppermute x2, waiting for transfers between devices, per_device(): passed = lax.ppermute(finished, 'section', onward)  10.4 us
    ppermute x2, starting transfers between devices, per_device(): passed = lax.ppermute(finished, 'section', onward)  3.84 us
    all_to_all x1, waiting for transfers between devices, exchanged(): return lax.all_to_all(value, axes, 0, 0, tiled=True)  3.66 us
    ppermute x1, starting transfers between devices, swapped(): return lax.ppermute(value, 'core', [(0, 1), (1, 0)])  2.99 us
  transfers between devices with their start and end apart: 4, of which 3 were waited for; matrix products, arithmetic and copies ran while one was open for 0% of the time, Pallas kernels for 3%

profile of v4, /device:TPU:1, one launch (start us, length us, event | category | flops | bytes accessed | tf_op | source)
XLA Modules:
  0.0 126.0 jit_solution(17412539791923171017)
XLA Ops:
  0.6 1.8 %shard_map.141 = bf16[8,144,128]{2,1,0:T(8,128)(2,1)} custom-call(bf16[128,128]{1,0:T(8,128)(2,1)} %bitcast.28, bf16[64,8,128]{2,1,0:T(8,128)(2,1)} %bitcast.26, bf16[64,8,128]{2,1,0:T(8,128)(2,1)} %bitcast.27), custom_call_target="tpu_custom_call" | custom-call | tf_op jit(solution)/shard_map/pallas_call | solution.py:288
  2.5 10.8 %all-to-all-start = ((bf16[8,144,128]{2,1,0:T(8,128)(2,1)}), bf16[8,144,128]{2,1,0:T(8,128)(2,1)}, u32[]{:S(2)}, u32[]{:S(2)}) async-start(bf16[8,144,128]{2,1,0:T(8,128)(2,1)} %shard_map.141), calls=%async_computation | async-start | bytes 589824 | tf_op jit(solution)/shard_map/all_to_all | solution.py:304
  13.9 2.0 %shard_map.140 = (bf16[432,4096]{1,0:T(8,128)(2,1)S(1)}, f32[8,128]{1,0:T(8,128)S(1)}) custom-call(f32[1,1]{1,0:T(1,128)S(6)} %copy.18.decay_ref, bf16[144,2,4096]{2,1,0:T(2,128)(2,1)} %bitcast.24, bf16[144,4096]{1,0:T(8,128)(2,1)} %bitcast.25), custom_call_target="tpu_custom_call" | custom-call | bytes 8388608 | tf_op jit(solution)/shard_map/pallas_call | solution.py:288
  16.0 0.6 copy-done.2
  16.6 3.7 %all-to-all-done.swapped_hbm = bf16[8,144,128]{2,1,0:T(8,128)(2,1)} async-done(((bf16[8,144,128]{2,1,0:T(8,128)(2,1)}), bf16[8,144,128]{2,1,0:T(8,128)(2,1)}, u32[]{:S(2)}, u32[]{:S(2)}) %all-to-all-start) | async-done | bytes 294944 | tf_op jit(solution)/shard_map/all_to_all | solution.py:304
  20.2 1.2 shard_map.142
  21.4 3.0 %collective-permute-start = (bf16[432,4096]{1,0:T(8,128)(2,1)S(1)}, bf16[432,4096]{1,0:T(8,128)(2,1)S(1)}, u32[]{:S(2)}, u32[]{:S(2)}) collective-permute-start(bf16[432,4096]{1,0:T(8,128)(2,1)S(1)} %get-tuple-element.29.near_ref), channel_id=1, source_target_pairs={{0,4},{4,0},{1,5},{5,1},{2,6},{6,2},{3,7},{7,3},{8,12},{12,8},{9,1... | collective-permute-start | bytes 10616840 | tf_op jit(solution)/shard_map/ppermute | solution.py:300
  24.4 6.6 %all_to_all.41 = f32[4,8,128]{2,1,0:T(8,128)S(1)} all-to-all(f32[4,8,128]{2,1,0:T(8,128)S(1)} %get-tuple-element.23), channel_id=1, replica_groups=mesh['section'=16,'x'=4,'core'=2,'tp'=4] {'tp'}, dimensions={0} | all-to-all | bytes 32768 | tf_op jit(solution)/shard_map/all_to_all | solution.py:304
  31.0 0.9 shard_map.143
  31.9 15.2 %all_to_all.42.rows_ref = bf16[32,64,128]{2,1,0:T(8,128)(2,1)S(1)} all-to-all(bf16[32,64,128]{2,1,0:T(8,128)(2,1)S(1)} %get-tuple-element.28), channel_id=1, replica_groups=mesh['section'=16,'x'=4,'core'=2,'tp'=4] {'x','core','tp'}, dimensions={0} | all-to-all | bytes 1048576 | tf_op jit(solution)/shard_map/all_to_all | solution.py:304
  47.1 2.0 %shard_map.144 = bf16[32,64,128]{2,1,0:T(8,128)(2,1)S(1)} custom-call(bf16[32,64,128]{2,1,0:T(8,128)(2,1)S(1)} %all_to_all.42.rows_ref, f32[1,4096]{1,0:T(1,128)S(1)} %copy-done, bf16[432,4096]{1,0:T(8,128)(2,1)S(1)} %get-tuple-element.29.near_ref, bf16[432,4096]{1,0:T(8,128)(2,1)S(1)} %collective-permute-done.far_ref), custom_call_target="tpu_custom_call" | custom-call | tf_op jit(solution)/shard_map/pallas_call | solution.py:288
  49.1 15.4 %all_to_all.43.parts_ref = bf16[32,64,128]{2,1,0:T(8,128)(2,1)S(1)} all-to-all(bf16[32,64,128]{2,1,0:T(8,128)(2,1)S(1)} %shard_map.144), channel_id=1, replica_groups=mesh['section'=16,'x'=4,'core'=2,'tp'=4] {'x','core','tp'}, dimensions={0} | all-to-all | bytes 1048576 | tf_op jit(solution)/shard_map/all_to_all | solution.py:304
  64.6 1.9 %collective-permute-start.1 = (bf16[128,128]{1,0:T(8,128)(2,1)S(1)}, bf16[128,128]{1,0:T(8,128)(2,1)S(1)}, u32[]{:S(2)}, u32[]{:S(2)}) collective-permute-start(bf16[128,128]{1,0:T(8,128)(2,1)S(1)} %shard_map.145), channel_id=1, source_target_pairs={{0,32},{32,64},{64,96},{96,128},{128,160},{160,192},{192,224},{224... | collective-permute-start | bytes 98312 | tf_op jit(solution)/shard_map/ppermute | solution.py:410
  66.5 7.4 %collective-permute-done.1.passed_ref = bf16[128,128]{1,0:T(8,128)(2,1)S(1)} collective-permute-done((bf16[128,128]{1,0:T(8,128)(2,1)S(1)}, bf16[128,128]{1,0:T(8,128)(2,1)S(1)}, u32[]{:S(2)}, u32[]{:S(2)}) %collective-permute-start.1) | collective-permute-done | bytes 32800 | tf_op jit(solution)/shard_map/ppermute | solution.py:410
  73.9 0.2 shard_map.146
  74.1 12.1 %all_to_all.44 = f32[32,1,128]{2,1,0:T(1,128)S(1)} all-to-all(f32[32,1,128]{2,1,0:T(1,128)S(1)} %bitcast.23), channel_id=1, replica_groups=mesh['section'=16,'x'=4,'core'=2,'tp'=4] {'x','core','tp'}, dimensions={0} | all-to-all | bytes 32768 | tf_op jit(solution)/shard_map/all_to_all | solution.py:304
  86.2 1.0 shard_map.147
  87.2 14.8 %all_to_all.45.rows_ref = bf16[32,64,128]{2,1,0:T(8,128)(2,1)S(1)} all-to-all(bf16[32,64,128]{2,1,0:T(8,128)(2,1)S(1)} %get-tuple-element.35), channel_id=1, replica_groups=mesh['section'=16,'x'=4,'core'=2,'tp'=4] {'x','core','tp'}, dimensions={0} | all-to-all | bytes 1048576 | tf_op jit(solution)/shard_map/all_to_all | solution.py:304
  102.0 2.0 %shard_map.148 = bf16[32,64,128]{2,1,0:T(8,128)(2,1)S(1)} custom-call(bf16[32,64,128]{2,1,0:T(8,128)(2,1)S(1)} %all_to_all.45.rows_ref, f32[1,4096]{1,0:T(1,128)S(1)} %copy-done, bf16[432,4096]{1,0:T(8,128)(2,1)S(1)} %get-tuple-element.29.near_ref, bf16[432,4096]{1,0:T(8,128)(2,1)S(1)} %collective-permute-done.far_ref), custom_call_target="tpu_custom_call" | custom-call | tf_op jit(solution)/shard_map/pallas_call | solution.py:288
  104.0 15.4 %all_to_all.46.parts_ref = bf16[32,64,128]{2,1,0:T(8,128)(2,1)S(1)} all-to-all(bf16[32,64,128]{2,1,0:T(8,128)(2,1)S(1)} %shard_map.148), channel_id=1, replica_groups=mesh['section'=16,'x'=4,'core'=2,'tp'=4] {'x','core','tp'}, dimensions={0} | all-to-all | bytes 1048576 | tf_op jit(solution)/shard_map/all_to_all | solution.py:304
  119.5 1.9 %collective-permute-start.2 = (bf16[128,128]{1,0:T(8,128)(2,1)S(1)}, bf16[128,128]{1,0:T(8,128)(2,1)S(1)}, u32[]{:S(2)}, u32[]{:S(2)}) collective-permute-start(bf16[128,128]{1,0:T(8,128)(2,1)S(1)} %shard_map.149), channel_id=1, source_target_pairs={{0,32},{32,64},{64,96},{96,128},{128,160},{160,192},{192,224},{224... | collective-permute-start | bytes 98312 | tf_op jit(solution)/shard_map/ppermute | solution.py:410
  121.4 0.9 shard_map.150
  122.3 3.0 %collective-permute-done.2 = bf16[128,128]{1,0:T(8,128)(2,1)S(1)} collective-permute-done((bf16[128,128]{1,0:T(8,128)(2,1)S(1)}, bf16[128,128]{1,0:T(8,128)(2,1)S(1)}, u32[]{:S(2)}, u32[]{:S(2)}) %collective-permute-start.2) | collective-permute-done | bytes 32800 | tf_op jit(solution)/shard_map/ppermute | solution.py:410
  125.3 0.6 maximum_bitcast_fusion
  (8 shorter events, 0.2 us)
Async XLA Ops:
  0.6 46.5 %copy-start = (f32[1,4096]{1,0:T(1,128)S(1)}, f32[1,4096]{1,0:T(1,128)}, u32[]{:S(2)}) copy-start(f32[1,4096]{1,0:T(1,128)} %gain_ref.3) | copy-start | bytes 49156
  2.5 17.8 %all-to-all-start = ((bf16[8,144,128]{2,1,0:T(8,128)(2,1)}), bf16[8,144,128]{2,1,0:T(8,128)(2,1)}, u32[]{:S(2)}, u32[]{:S(2)}) async-start(bf16[8,144,128]{2,1,0:T(8,128)(2,1)} %shard_map.141), calls=%async_computation | async-start | bytes 589824 | tf_op jit(solution)/shard_map/all_to_all | solution.py:304
  16.0 0.6 copy-start.2
  21.4 25.7 %collective-permute-start = (bf16[432,4096]{1,0:T(8,128)(2,1)S(1)}, bf16[432,4096]{1,0:T(8,128)(2,1)S(1)}, u32[]{:S(2)}, u32[]{:S(2)}) collective-permute-start(bf16[432,4096]{1,0:T(8,128)(2,1)S(1)} %get-tuple-element.29.near_ref), channel_id=1, source_target_pairs={{0,4},{4,0},{1,5},{5,1},{2,6},{6,2},{3,7},{7,3},{8,12},{12,8},{9,1... | collective-permute-start | bytes 10616840 | tf_op jit(solution)/shard_map/ppermute | solution.py:300
  47.1 26.8 %copy-start.1 = (bf16[1,128,128]{2,1,0:T(8,128)(2,1)S(1)}, bf16[1,128,128]{2,1,0:T(8,128)(2,1)}, u32[]{:S(2)}) copy-start(bf16[1,128,128]{2,1,0:T(8,128)(2,1)} %param.14) | copy-start | bytes 98308
  64.6 9.3 %collective-permute-start.1 = (bf16[128,128]{1,0:T(8,128)(2,1)S(1)}, bf16[128,128]{1,0:T(8,128)(2,1)S(1)}, u32[]{:S(2)}, u32[]{:S(2)}) collective-permute-start(bf16[128,128]{1,0:T(8,128)(2,1)S(1)} %shard_map.145), channel_id=1, source_target_pairs={{0,32},{32,64},{64,96},{96,128},{128,160},{160,192},{192,224},{224... | collective-permute-start | bytes 98312 | tf_op jit(solution)/shard_map/ppermute | solution.py:410
  119.5 5.9 %collective-permute-start.2 = (bf16[128,128]{1,0:T(8,128)(2,1)S(1)}, bf16[128,128]{1,0:T(8,128)(2,1)S(1)}, u32[]{:S(2)}, u32[]{:S(2)}) collective-permute-start(bf16[128,128]{1,0:T(8,128)(2,1)S(1)} %shard_map.149), channel_id=1, source_target_pairs={{0,32},{32,64},{64,96},{96,128},{128,160},{160,192},{192,224},{224... | collective-permute-start | bytes 98312 | tf_op jit(solution)/shard_map/ppermute | solution.py:410

commit v5 on v4

--- a/solution.py
+++ b/solution.py
@@ -22,6 +22,7 @@
 EPS = 1e-6
 MASKED = -1e30
 SECTION = ("x", "core", "tp")
+PEERS = ("core", "x", "tp")
 F32 = jnp.float32
 BF16 = jnp.bfloat16
 HIGH = lax.Precision.HIGHEST
@@ -31,6 +32,10 @@
     return lax.dot_general(
         left, right, ((dims[:1], dims[1:]), ((), ())), precision=precision, preferred_element_type=F32
     )
+
+
+def peer(block):
+    return block // 4 % 2 * 16 + block // 8 * 4 + block % 4
 
 
 def block_place():
@@ -208,7 +213,7 @@
     mixed_ref[...] = mixed
     for block in range(BLOCKS):
         half = block // 4 % 2
-        spread_ref[block] = mixed[half * HALF : (half + 1) * HALF]
+        spread_ref[peer(block)] = mixed[half * HALF : (half + 1) * HALF]
 
 
 def feed_kernel(rows_ref, gain_ref, near_ref, far_ref, out_ref, wide_ref):
@@ -219,7 +224,7 @@
         place = slice(first, first + step)
         pieces = []
         for block in range(first // HEAD, (first + step) // HEAD):
-            rows = rows_ref[block].astype(F32)
+            rows = rows_ref[peer(block)].astype(F32)
             squares = squares + rows * rows
             gain = gain_ref[:, block * HEAD : (block + 1) * HEAD]
             pieces.append((rows * gain).astype(BF16))
@@ -240,7 +245,7 @@
             hidden[1], far_ref[2 * UNITS :, place], (1, 0)
         )
         for block in range(step // HEAD):
-            out_ref[first // HEAD + block] = down[:, block * HEAD : (block + 1) * HEAD].astype(BF16)
+            out_ref[peer(first // HEAD + block)] = down[:, block * HEAD : (block + 1) * HEAD].astype(BF16)
 
 
 def prepare_kernel(decay_ref, gate_up_hbm, down_hbm, weights_ref, decays_ref, raw_ref, sems):
@@ -267,9 +272,8 @@
     for half in range(2):
         place = slice(half * HALF, (half + 1) * HALF)
         total = mixed_ref[place].astype(F32)
-        for block in range(BLOCKS):
-            if block // 4 % 2 == half:
-                total = total + parts_ref[block].astype(F32)
+        for chip in range(BLOCKS // 2):
+            total = total + parts_ref[half * (BLOCKS // 2) + chip].astype(F32)
         out_ref[place] = total.astype(BF16)
 
 
@@ -300,7 +304,7 @@
     return lax.ppermute(value, "core", [(0, 1), (1, 0)])
 
 
-def exchanged(value, axes=SECTION):
+def exchanged(value, axes=PEERS):
     return lax.all_to_all(value, axes, 0, 0, tiled=True)
 
 

time: 127 us -> 126 us (level)
  no operation moved by 1% of the time
where the time goes in v5:
time: 126 us; the launch traced here: 125 us
  blocking collectives  78.6 us (62%)
  starting transfers between devices  17.7 us (14%)
  waiting for transfers between devices  14.1 us (11%)
  Pallas kernels  12.2 us (10%)
  between operations  1.39 us (1%)
    all_to_all x6, blocking collectives, exchanged(): return lax.all_to_all(value, axes, 0, 0, tiled=True)  78.6 us
    pallas_call x11, Pallas kernels, local_call(): pl.pallas_call(kernel, out_shape=outs, in_specs=[pl.BlockSpec(memory_spac...  12.2 us
    all_to_all x1, starting transfers between devices, exchanged(): return lax.all_to_all(value, axes, 0, 0, tiled=True)  10.8 us
    ppermute x2, waiting for transfers between devices, per_device(): passed = lax.ppermute(finished, 'section', onward)  10.4 us
    ppermute x2, starting transfers between devices, per_device(): passed = lax.ppermute(finished, 'section', onward)  3.84 us
    all_to_all x1, waiting for transfers between devices, exchanged(): return lax.all_to_all(value, axes, 0, 0, tiled=True)  3.66 us
    ppermute x1, starting transfers between devices, swapped(): return lax.ppermute(value, 'core', [(0, 1), (1, 0)])  2.99 us
  transfers between devices with their start and end apart: 4, of which 3 were waited for; matrix products, arithmetic and copies ran while one was open for 0% of the time, Pallas kernels for 3%

profile of v5, /device:TPU:1, one launch (start us, length us, event | category | flops | bytes accessed | tf_op | source)
XLA Modules:
  0.0 125.2 jit_solution(1711526288957621807)
XLA Ops:
  0.6 1.8 %shard_map.141 = bf16[8,144,128]{2,1,0:T(8,128)(2,1)} custom-call(bf16[128,128]{1,0:T(8,128)(2,1)} %bitcast.28, bf16[64,8,128]{2,1,0:T(8,128)(2,1)} %bitcast.26, bf16[64,8,128]{2,1,0:T(8,128)(2,1)} %bitcast.27), custom_call_target="tpu_custom_call" | custom-call | tf_op jit(solution)/shard_map/pallas_call | solution.py:292
  2.5 10.8 %all-to-all-start = ((bf16[8,144,128]{2,1,0:T(8,128)(2,1)}), bf16[8,144,128]{2,1,0:T(8,128)(2,1)}, u32[]{:S(2)}, u32[]{:S(2)}) async-start(bf16[8,144,128]{2,1,0:T(8,128)(2,1)} %shard_map.141), calls=%async_computation | async-start | bytes 589824 | tf_op jit(solution)/shard_map/all_to_all | solution.py:308
  13.9 2.0 %shard_map.140 = (bf16[432,4096]{1,0:T(8,128)(2,1)S(1)}, f32[8,128]{1,0:T(8,128)S(1)}) custom-call(f32[1,1]{1,0:T(1,128)S(6)} %copy.18.decay_ref, bf16[144,2,4096]{2,1,0:T(2,128)(2,1)} %bitcast.24, bf16[144,4096]{1,0:T(8,128)(2,1)} %bitcast.25), custom_call_target="tpu_custom_call" | custom-call | bytes 8388608 | tf_op jit(solution)/shard_map/pallas_call | solution.py:292
  16.0 0.6 copy-done.2
  16.6 3.7 %all-to-all-done.swapped_hbm = bf16[8,144,128]{2,1,0:T(8,128)(2,1)} async-done(((bf16[8,144,128]{2,1,0:T(8,128)(2,1)}), bf16[8,144,128]{2,1,0:T(8,128)(2,1)}, u32[]{:S(2)}, u32[]{:S(2)}) %all-to-all-start) | async-done | bytes 294944 | tf_op jit(solution)/shard_map/all_to_all | solution.py:308
  20.2 1.2 shard_map.142
  21.4 3.0 %collective-permute-start = (bf16[432,4096]{1,0:T(8,128)(2,1)S(1)}, bf16[432,4096]{1,0:T(8,128)(2,1)S(1)}, u32[]{:S(2)}, u32[]{:S(2)}) collective-permute-start(bf16[432,4096]{1,0:T(8,128)(2,1)S(1)} %get-tuple-element.29.near_ref), channel_id=1, source_target_pairs={{0,4},{4,0},{1,5},{5,1},{2,6},{6,2},{3,7},{7,3},{8,12},{12,8},{9,1... | collective-permute-start | bytes 10616840 | tf_op jit(solution)/shard_map/ppermute | solution.py:304
  24.4 6.6 %all_to_all.41 = f32[4,8,128]{2,1,0:T(8,128)S(1)} all-to-all(f32[4,8,128]{2,1,0:T(8,128)S(1)} %get-tuple-element.23), channel_id=1, replica_groups=mesh['section'=16,'x'=4,'core'=2,'tp'=4] {'tp'}, dimensions={0} | all-to-all | bytes 32768 | tf_op jit(solution)/shard_map/all_to_all | solution.py:308
  31.0 0.9 shard_map.143
  31.9 15.3 %all_to_all.42.rows_ref = bf16[32,64,128]{2,1,0:T(8,128)(2,1)S(1)} all-to-all(bf16[32,64,128]{2,1,0:T(8,128)(2,1)S(1)} %get-tuple-element.28), channel_id=1, replica_groups=mesh['section'=16,'x'=4,'core'=2,'tp'=4] {'core','x','tp'}, dimensions={0} | all-to-all | bytes 1048576 | tf_op jit(solution)/shard_map/all_to_all | solution.py:308
  47.3 2.0 %shard_map.144 = bf16[32,64,128]{2,1,0:T(8,128)(2,1)S(1)} custom-call(bf16[32,64,128]{2,1,0:T(8,128)(2,1)S(1)} %all_to_all.42.rows_ref, f32[1,4096]{1,0:T(1,128)S(1)} %copy-done, bf16[432,4096]{1,0:T(8,128)(2,1)S(1)} %get-tuple-element.29.near_ref, bf16[432,4096]{1,0:T(8,128)(2,1)S(1)} %collective-permute-done.far_ref), custom_call_target="tpu_custom_call" | custom-call | tf_op jit(solution)/shard_map/pallas_call | solution.py:292
  49.3 15.1 %all_to_all.43.parts_ref = bf16[32,64,128]{2,1,0:T(8,128)(2,1)S(1)} all-to-all(bf16[32,64,128]{2,1,0:T(8,128)(2,1)S(1)} %shard_map.144), channel_id=1, replica_groups=mesh['section'=16,'x'=4,'core'=2,'tp'=4] {'core','x','tp'}, dimensions={0} | all-to-all | bytes 1048576 | tf_op jit(solution)/shard_map/all_to_all | solution.py:308
  64.4 1.9 %collective-permute-start.1 = (bf16[128,128]{1,0:T(8,128)(2,1)S(1)}, bf16[128,128]{1,0:T(8,128)(2,1)S(1)}, u32[]{:S(2)}, u32[]{:S(2)}) collective-permute-start(bf16[128,128]{1,0:T(8,128)(2,1)S(1)} %shard_map.145), channel_id=1, source_target_pairs={{0,32},{32,64},{64,96},{96,128},{128,160},{160,192},{192,224},{224... | collective-permute-start | bytes 98312 | tf_op jit(solution)/shard_map/ppermute | solution.py:414
  66.4 7.4 %collective-permute-done.1.passed_ref = bf16[128,128]{1,0:T(8,128)(2,1)S(1)} collective-permute-done((bf16[128,128]{1,0:T(8,128)(2,1)S(1)}, bf16[128,128]{1,0:T(8,128)(2,1)S(1)}, u32[]{:S(2)}, u32[]{:S(2)}) %collective-permute-start.1) | collective-permute-done | bytes 32800 | tf_op jit(solution)/shard_map/ppermute | solution.py:414
  73.8 0.2 shard_map.146
  74.0 11.6 %all_to_all.44 = f32[32,1,128]{2,1,0:T(1,128)S(1)} all-to-all(f32[32,1,128]{2,1,0:T(1,128)S(1)} %bitcast.23), channel_id=1, replica_groups=mesh['section'=16,'x'=4,'core'=2,'tp'=4] {'core','x','tp'}, dimensions={0} | all-to-all | bytes 32768 | tf_op jit(solution)/shard_map/all_to_all | solution.py:308
  85.6 1.0 shard_map.147
  86.6 14.9 %all_to_all.45.rows_ref = bf16[32,64,128]{2,1,0:T(8,128)(2,1)S(1)} all-to-all(bf16[32,64,128]{2,1,0:T(8,128)(2,1)S(1)} %get-tuple-element.35), channel_id=1, replica_groups=mesh['section'=16,'x'=4,'core'=2,'tp'=4] {'core','x','tp'}, dimensions={0} | all-to-all | bytes 1048576 | tf_op jit(solution)/shard_map/all_to_all | solution.py:308
  101.5 2.0 %shard_map.148 = bf16[32,64,128]{2,1,0:T(8,128)(2,1)S(1)} custom-call(bf16[32,64,128]{2,1,0:T(8,128)(2,1)S(1)} %all_to_all.45.rows_ref, f32[1,4096]{1,0:T(1,128)S(1)} %copy-done, bf16[432,4096]{1,0:T(8,128)(2,1)S(1)} %get-tuple-element.29.near_ref, bf16[432,4096]{1,0:T(8,128)(2,1)S(1)} %collective-permute-done.far_ref), custom_call_target="tpu_custom_call" | custom-call | tf_op jit(solution)/shard_map/pallas_call | solution.py:292
  103.5 15.1 %all_to_all.46.parts_ref = bf16[32,64,128]{2,1,0:T(8,128)(2,1)S(1)} all-to-all(bf16[32,64,128]{2,1,0:T(8,128)(2,1)S(1)} %shard_map.148), channel_id=1, replica_groups=mesh['section'=16,'x'=4,'core'=2,'tp'=4] {'core','x','tp'}, dimensions={0} | all-to-all | bytes 1048576 | tf_op jit(solution)/shard_map/all_to_all | solution.py:308
  118.7 1.9 %collective-permute-start.2 = (bf16[128,128]{1,0:T(8,128)(2,1)S(1)}, bf16[128,128]{1,0:T(8,128)(2,1)S(1)}, u32[]{:S(2)}, u32[]{:S(2)}) collective-permute-start(bf16[128,128]{1,0:T(8,128)(2,1)S(1)} %shard_map.149), channel_id=1, source_target_pairs={{0,32},{32,64},{64,96},{96,128},{128,160},{160,192},{192,224},{224... | collective-permute-start | bytes 98312 | tf_op jit(solution)/shard_map/ppermute | solution.py:414
  120.6 0.9 shard_map.150
  121.5 3.0 %collective-permute-done.2 = bf16[128,128]{1,0:T(8,128)(2,1)S(1)} collective-permute-done((bf16[128,128]{1,0:T(8,128)(2,1)S(1)}, bf16[128,128]{1,0:T(8,128)(2,1)S(1)}, u32[]{:S(2)}, u32[]{:S(2)}) %collective-permute-start.2) | collective-permute-done | bytes 32800 | tf_op jit(solution)/shard_map/ppermute | solution.py:414
  124.6 0.6 maximum_bitcast_fusion
  (8 shorter events, 0.2 us)
Async XLA Ops:
  0.6 46.6 %copy-start = (f32[1,4096]{1,0:T(1,128)S(1)}, f32[1,4096]{1,0:T(1,128)}, u32[]{:S(2)}) copy-start(f32[1,4096]{1,0:T(1,128)} %gain_ref.3) | copy-start | bytes 49156
  2.5 17.8 %all-to-all-start = ((bf16[8,144,128]{2,1,0:T(8,128)(2,1)}), bf16[8,144,128]{2,1,0:T(8,128)(2,1)}, u32[]{:S(2)}, u32[]{:S(2)}) async-start(bf16[8,144,128]{2,1,0:T(8,128)(2,1)} %shard_map.141), calls=%async_computation | async-start | bytes 589824 | tf_op jit(solution)/shard_map/all_to_all | solution.py:308
  16.0 0.6 copy-start.2
  21.4 25.9 %collective-permute-start = (bf16[432,4096]{1,0:T(8,128)(2,1)S(1)}, bf16[432,4096]{1,0:T(8,128)(2,1)S(1)}, u32[]{:S(2)}, u32[]{:S(2)}) collective-permute-start(bf16[432,4096]{1,0:T(8,128)(2,1)S(1)} %get-tuple-element.29.near_ref), channel_id=1, source_target_pairs={{0,4},{4,0},{1,5},{5,1},{2,6},{6,2},{3,7},{7,3},{8,12},{12,8},{9,1... | collective-permute-start | bytes 10616840 | tf_op jit(solution)/shard_map/ppermute | solution.py:304
  47.3 26.5 %copy-start.1 = (bf16[1,128,128]{2,1,0:T(8,128)(2,1)S(1)}, bf16[1,128,128]{2,1,0:T(8,128)(2,1)}, u32[]{:S(2)}) copy-start(bf16[1,128,128]{2,1,0:T(8,128)(2,1)} %param.14) | copy-start | bytes 98308
  64.4 9.3 %collective-permute-start.1 = (bf16[128,128]{1,0:T(8,128)(2,1)S(1)}, bf16[128,128]{1,0:T(8,128)(2,1)S(1)}, u32[]{:S(2)}, u32[]{:S(2)}) collective-permute-start(bf16[128,128]{1,0:T(8,128)(2,1)S(1)} %shard_map.145), channel_id=1, source_target_pairs={{0,32},{32,64},{64,96},{96,128},{128,160},{160,192},{192,224},{224... | collective-permute-start | bytes 98312 | tf_op jit(solution)/shard_map/ppermute | solution.py:414
  118.7 5.9 %collective-permute-start.2 = (bf16[128,128]{1,0:T(8,128)(2,1)S(1)}, bf16[128,128]{1,0:T(8,128)(2,1)S(1)}, u32[]{:S(2)}, u32[]{:S(2)}) collective-permute-start(bf16[128,128]{1,0:T(8,128)(2,1)S(1)} %shard_map.149), channel_id=1, source_target_pairs={{0,32},{32,64},{64,96},{96,128},{128,160},{160,192},{192,224},{224... | collective-permute-start | bytes 98312 | tf_op jit(solution)/shard_map/ppermute | solution.py:414

commit v6 on v5

--- a/solution.py
+++ b/solution.py
@@ -38,6 +38,19 @@
     return block // 4 % 2 * 16 + block // 8 * 4 + block % 4
 
 
+def pieces(value, count, axis):
+    parts = []
+    for _ in range(count):
+        parts.append(value.astype(BF16))
+        value = value - parts[-1].astype(F32)
+    return jnp.concatenate(parts, axis=axis)
+
+
+def lane_sums(values, count, rows):
+    split = pieces(values, count, 1)
+    return dot(jnp.ones((rows, split.shape[1]), BF16), split, (1, 1))
+
+
 def block_place():
     return (lax.axis_index("x") * 2 + lax.axis_index("core")) * 4 + lax.axis_index("tp")
 
@@ -45,7 +58,7 @@
 def write_square_sums(rows, parts_ref):
     squares = rows.astype(F32)
     squares = squares * squares
-    sums = dot(jnp.ones((8, HEAD), F32), squares, (1, 1), HIGH)
+    sums = lane_sums(squares, 2, 8)
     parts_ref[...] = jnp.concatenate([sums] * (BLOCKS // 8), axis=0)
 
 
@@ -63,7 +76,7 @@
     copies[0].wait()
     squares = rows_ref[...].astype(F32)
     squares = squares * squares
-    sums = dot(jnp.ones((TAIL, HEAD), F32), squares, (1, 1), HIGH)
+    sums = lane_sums(squares, 2, TAIL)
     high = sums.astype(BF16).astype(F32)
     middle = (sums - high).astype(BF16).astype(F32)
     row = lax.broadcasted_iota(jnp.int32, (TAIL, HEAD), 0)
@@ -74,7 +87,7 @@
         by_head = jnp.swapaxes(ref[...], 0, 1)
         span = pl.ds(index * ROWS, ROWS)
         for shard in range(SHARDS):
-            out_ref[shard, span] = by_head[shard]
+            out_ref[shard, span] = by_head[shard % 4 * 2 + shard // 4]
             if index:
                 out_ref[shard, 2 * ROWS :] = tail
         span = pl.ds(index * ROWS, ROWS + index * TAIL)
@@ -133,7 +146,8 @@
     slot = lax.broadcasted_iota(jnp.int32, (1, SHARDS * ROWS), 1)
     used = jnp.zeros((1, SHARDS * ROWS), jnp.int32)
     for shard in range(SHARDS):
-        used = jnp.where(slot // ROWS == shard, lengths_ref[0, shard], used)
+        length = lengths_ref[0, shard % 4 * 2 + shard // 4]
+        used = jnp.where(slot // ROWS == shard, length, used)
     consts_ref[0:1] = jnp.where(slot % ROWS < used, 0.0, MASKED)
     for index in range(3):
         consts_ref[1:2, index * HEAD : (index + 1) * HEAD] = gains_ref[index]
@@ -165,7 +179,8 @@
     gain, key_gain, linear_gain, decay = [
         consts_ref[1:2, index * HEAD : (index + 1) * HEAD] for index in range(4)
     ]
-    sums = dot(parts_ref[...], jnp.ones((BLOCKS, HEAD), F32), (0, 0), HIGH)
+    parts = pieces(parts_ref[...], 3, 0)
+    sums = dot(parts, jnp.ones(parts.shape, BF16), (0, 0))
     rows = rows_ref[...].astype(F32)
     normed = rows * lax.rsqrt(sums * (1.0 / DIM) + EPS) * gain
     queries = normed.astype(BF16)
@@ -231,7 +246,7 @@
         feed = jnp.concatenate(pieces, axis=1)
         for side, ref in enumerate((near_ref, far_ref)):
             sums[side] = sums[side] + dot(ref[: 2 * UNITS, place], feed, (1, 1))
-    mean = dot(jnp.ones((8, HEAD), F32), squares, (1, 1), HIGH)[:1] * (1.0 / DIM)
+    mean = lane_sums(squares, 3, 8)[:1] * (1.0 / DIM)
     factor = lax.rsqrt(mean + EPS)
     hidden = []
     for side in range(2):
@@ -338,7 +353,7 @@
         spaces=dict.fromkeys(range(3), pltpu.HBM),
         out_space=pltpu.HBM,
     )
-    sent = exchanged(sent, ("x", "core"))
+    sent = exchanged(sent, ("core", "x"))
     weights, decays = local_call(
         prepare_kernel,
         (shape_of(3 * UNITS, DIM), shape_of(8, HEAD, dtype=F32)),

time: 126 us -> 125 us (level)
  no operation moved by 1% of the time
where the time goes in v6:
time: 125 us
  blocking collectives  79.2 us (63%)
  starting transfers between devices  17 us (14%)
  waiting for transfers between devices  14.2 us (11%)
  Pallas kernels  11.7 us (9%)
  between operations  1.39 us (1%)
    all_to_all x6, blocking collectives, exchanged(): return lax.all_to_all(value, axes, 0, 0, tiled=True)  79.2 us
    pallas_call x11, Pallas kernels, local_call(): pl.pallas_call(kernel, out_shape=outs, in_specs=[pl.BlockSpec(memory_spac...  11.7 us
    all_to_all x1, starting transfers between devices, exchanged(): return lax.all_to_all(value, axes, 0, 0, tiled=True)  10.8 us
    ppermute x2, waiting for transfers between devices, per_device(): passed = lax.ppermute(finished, 'section', onward)  10.4 us
    ppermute x2, starting transfers between devices, per_device(): passed = lax.ppermute(finished, 'section', onward)  3.84 us
    all_to_all x1, waiting for transfers between devices, exchanged(): return lax.all_to_all(value, axes, 0, 0, tiled=True)  3.74 us
  transfers between devices with their start and end apart: 4, of which 3 were waited for; matrix products, arithmetic and copies ran while one was open for 0% of the time, Pallas kernels for 3%

profile of v6, /device:TPU:1, one launch (start us, length us, event | category | flops | bytes accessed | tf_op | source)
XLA Modules:
  0.0 124.7 jit_solution(17243809106683005380)
XLA Ops:
  0.6 1.7 %shard_map.141 = bf16[8,144,128]{2,1,0:T(8,128)(2,1)} custom-call(bf16[128,128]{1,0:T(8,128)(2,1)} %bitcast.28, bf16[64,8,128]{2,1,0:T(8,128)(2,1)} %bitcast.26, bf16[64,8,128]{2,1,0:T(8,128)(2,1)} %bitcast.27), custom_call_target="tpu_custom_call" | custom-call | tf_op jit(solution)/shard_map/pallas_call | solution.py:307
  2.4 10.8 %all-to-all-start = ((bf16[8,144,128]{2,1,0:T(8,128)(2,1)}), bf16[8,144,128]{2,1,0:T(8,128)(2,1)}, u32[]{:S(2)}, u32[]{:S(2)}) async-start(bf16[8,144,128]{2,1,0:T(8,128)(2,1)} %shard_map.141), calls=%async_computation | async-start | bytes 589824 | tf_op jit(solution)/shard_map/all_to_all | solution.py:323
  13.9 2.0 %shard_map.140 = (bf16[432,4096]{1,0:T(8,128)(2,1)S(1)}, f32[8,128]{1,0:T(8,128)S(1)}) custom-call(f32[1,1]{1,0:T(1,128)S(6)} %copy.18.decay_ref, bf16[144,2,4096]{2,1,0:T(2,128)(2,1)} %bitcast.24, bf16[144,4096]{1,0:T(8,128)(2,1)} %bitcast.25), custom_call_target="tpu_custom_call" | custom-call | bytes 8388608 | tf_op jit(solution)/shard_map/pallas_call | solution.py:307
  15.9 0.6 copy-done.2
  16.5 3.7 %all-to-all-done.swapped_hbm = bf16[8,144,128]{2,1,0:T(8,128)(2,1)} async-done(((bf16[8,144,128]{2,1,0:T(8,128)(2,1)}), bf16[8,144,128]{2,1,0:T(8,128)(2,1)}, u32[]{:S(2)}, u32[]{:S(2)}) %all-to-all-start) | async-done | bytes 294944 | tf_op jit(solution)/shard_map/all_to_all | solution.py:323
  20.3 1.2 shard_map.142
  21.4 2.3 %collective-permute-start = (bf16[432,4096]{1,0:T(8,128)(2,1)S(1)}, bf16[432,4096]{1,0:T(8,128)(2,1)S(1)}, u32[]{:S(2)}, u32[]{:S(2)}) collective-permute-start(bf16[432,4096]{1,0:T(8,128)(2,1)S(1)} %get-tuple-element.29.near_ref), channel_id=1, source_target_pairs={{0,4},{4,0},{1,5},{5,1},{2,6},{6,2},{3,7},{7,3},{8,12},{12,8},{9,1... | collective-permute-start | bytes 10616840 | tf_op jit(solution)/shard_map/ppermute | solution.py:319
  23.7 6.6 %all_to_all.41 = f32[4,8,128]{2,1,0:T(8,128)S(1)} all-to-all(f32[4,8,128]{2,1,0:T(8,128)S(1)} %get-tuple-element.23), channel_id=1, replica_groups=mesh['section'=16,'x'=4,'core'=2,'tp'=4] {'tp'}, dimensions={0} | all-to-all | bytes 32768 | tf_op jit(solution)/shard_map/all_to_all | solution.py:323
  30.3 0.8 shard_map.143
  31.1 16.0 %all_to_all.42.rows_ref = bf16[32,64,128]{2,1,0:T(8,128)(2,1)S(1)} all-to-all(bf16[32,64,128]{2,1,0:T(8,128)(2,1)S(1)} %get-tuple-element.28), channel_id=1, replica_groups=mesh['section'=16,'x'=4,'core'=2,'tp'=4] {'core','x','tp'}, dimensions={0} | all-to-all | bytes 1048576 | tf_op jit(solution)/shard_map/all_to_all | solution.py:323
  47.1 1.9 %shard_map.144 = bf16[32,64,128]{2,1,0:T(8,128)(2,1)S(1)} custom-call(bf16[32,64,128]{2,1,0:T(8,128)(2,1)S(1)} %all_to_all.42.rows_ref, f32[1,4096]{1,0:T(1,128)S(1)} %copy-done, bf16[432,4096]{1,0:T(8,128)(2,1)S(1)} %get-tuple-element.29.near_ref, bf16[432,4096]{1,0:T(8,128)(2,1)S(1)} %collective-permute-done.far_ref), custom_call_target="tpu_custom_call" | custom-call | tf_op jit(solution)/shard_map/pallas_call | solution.py:307
  49.0 15.1 %all_to_all.43.parts_ref = bf16[32,64,128]{2,1,0:T(8,128)(2,1)S(1)} all-to-all(bf16[32,64,128]{2,1,0:T(8,128)(2,1)S(1)} %shard_map.144), channel_id=1, replica_groups=mesh['section'=16,'x'=4,'core'=2,'tp'=4] {'core','x','tp'}, dimensions={0} | all-to-all | bytes 1048576 | tf_op jit(solution)/shard_map/all_to_all | solution.py:323
  64.2 1.9 %collective-permute-start.1 = (bf16[128,128]{1,0:T(8,128)(2,1)S(1)}, bf16[128,128]{1,0:T(8,128)(2,1)S(1)}, u32[]{:S(2)}, u32[]{:S(2)}) collective-permute-start(bf16[128,128]{1,0:T(8,128)(2,1)S(1)} %shard_map.145), channel_id=1, source_target_pairs={{0,32},{32,64},{64,96},{96,128},{128,160},{160,192},{192,224},{224... | collective-permute-start | bytes 98312 | tf_op jit(solution)/shard_map/ppermute | solution.py:429
  66.1 7.4 %collective-permute-done.1.passed_ref = bf16[128,128]{1,0:T(8,128)(2,1)S(1)} collective-permute-done((bf16[128,128]{1,0:T(8,128)(2,1)S(1)}, bf16[128,128]{1,0:T(8,128)(2,1)S(1)}, u32[]{:S(2)}, u32[]{:S(2)}) %collective-permute-start.1) | collective-permute-done | bytes 32800 | tf_op jit(solution)/shard_map/ppermute | solution.py:429
  73.5 0.1 shard_map.146
  73.7 11.6 %all_to_all.44 = f32[32,1,128]{2,1,0:T(1,128)S(1)} all-to-all(f32[32,1,128]{2,1,0:T(1,128)S(1)} %bitcast.23), channel_id=1, replica_groups=mesh['section'=16,'x'=4,'core'=2,'tp'=4] {'core','x','tp'}, dimensions={0} | all-to-all | bytes 32768 | tf_op jit(solution)/shard_map/all_to_all | solution.py:323
  85.3 0.9 shard_map.147
  86.2 14.9 %all_to_all.45.rows_ref = bf16[32,64,128]{2,1,0:T(8,128)(2,1)S(1)} all-to-all(bf16[32,64,128]{2,1,0:T(8,128)(2,1)S(1)} %get-tuple-element.35), channel_id=1, replica_groups=mesh['section'=16,'x'=4,'core'=2,'tp'=4] {'core','x','tp'}, dimensions={0} | all-to-all | bytes 1048576 | tf_op jit(solution)/shard_map/all_to_all | solution.py:323
  101.1 1.9 %shard_map.148 = bf16[32,64,128]{2,1,0:T(8,128)(2,1)S(1)} custom-call(bf16[32,64,128]{2,1,0:T(8,128)(2,1)S(1)} %all_to_all.45.rows_ref, f32[1,4096]{1,0:T(1,128)S(1)} %copy-done, bf16[432,4096]{1,0:T(8,128)(2,1)S(1)} %get-tuple-element.29.near_ref, bf16[432,4096]{1,0:T(8,128)(2,1)S(1)} %collective-permute-done.far_ref), custom_call_target="tpu_custom_call" | custom-call | tf_op jit(solution)/shard_map/pallas_call | solution.py:307
  103.0 15.1 %all_to_all.46.parts_ref = bf16[32,64,128]{2,1,0:T(8,128)(2,1)S(1)} all-to-all(bf16[32,64,128]{2,1,0:T(8,128)(2,1)S(1)} %shard_map.148), channel_id=1, replica_groups=mesh['section'=16,'x'=4,'core'=2,'tp'=4] {'core','x','tp'}, dimensions={0} | all-to-all | bytes 1048576 | tf_op jit(solution)/shard_map/all_to_all | solution.py:323
  118.2 1.9 %collective-permute-start.2 = (bf16[128,128]{1,0:T(8,128)(2,1)S(1)}, bf16[128,128]{1,0:T(8,128)(2,1)S(1)}, u32[]{:S(2)}, u32[]{:S(2)}) collective-permute-start(bf16[128,128]{1,0:T(8,128)(2,1)S(1)} %shard_map.149), channel_id=1, source_target_pairs={{0,32},{32,64},{64,96},{96,128},{128,160},{160,192},{192,224},{224... | collective-permute-start | bytes 98312 | tf_op jit(solution)/shard_map/ppermute | solution.py:429
  120.1 0.9 shard_map.150
  121.0 3.0 %collective-permute-done.2 = bf16[128,128]{1,0:T(8,128)(2,1)S(1)} collective-permute-done((bf16[128,128]{1,0:T(8,128)(2,1)S(1)}, bf16[128,128]{1,0:T(8,128)(2,1)S(1)}, u32[]{:S(2)}, u32[]{:S(2)}) %collective-permute-start.2) | collective-permute-done | bytes 32800 | tf_op jit(solution)/shard_map/ppermute | solution.py:429
  124.1 0.6 maximum_bitcast_fusion
  (8 shorter events, 0.2 us)
Async XLA Ops:
  0.6 46.5 %copy-start = (f32[1,4096]{1,0:T(1,128)S(1)}, f32[1,4096]{1,0:T(1,128)}, u32[]{:S(2)}) copy-start(f32[1,4096]{1,0:T(1,128)} %gain_ref.3) | copy-start | bytes 49156
  2.4 17.9 %all-to-all-start = ((bf16[8,144,128]{2,1,0:T(8,128)(2,1)}), bf16[8,144,128]{2,1,0:T(8,128)(2,1)}, u32[]{:S(2)}, u32[]{:S(2)}) async-start(bf16[8,144,128]{2,1,0:T(8,128)(2,1)} %shard_map.141), calls=%async_computation | async-start | bytes 589824 | tf_op jit(solution)/shard_map/all_to_all | solution.py:323
  15.9 0.6 copy-start.2
  21.4 25.7 %collective-permute-start = (bf16[432,4096]{1,0:T(8,128)(2,1)S(1)}, bf16[432,4096]{1,0:T(8,128)(2,1)S(1)}, u32[]{:S(2)}, u32[]{:S(2)}) collective-permute-start(bf16[432,4096]{1,0:T(8,128)(2,1)S(1)} %get-tuple-element.29.near_ref), channel_id=1, source_target_pairs={{0,4},{4,0},{1,5},{5,1},{2,6},{6,2},{3,7},{7,3},{8,12},{12,8},{9,1... | collective-permute-start | bytes 10616840 | tf_op jit(solution)/shard_map/ppermute | solution.py:319
  47.1 26.4 %copy-start.1 = (bf16[1,128,128]{2,1,0:T(8,128)(2,1)S(1)}, bf16[1,128,128]{2,1,0:T(8,128)(2,1)}, u32[]{:S(2)}) copy-start(bf16[1,128,128]{2,1,0:T(8,128)(2,1)} %param.14) | copy-start | bytes 98308
  64.2 9.3 %collective-permute-start.1 = (bf16[128,128]{1,0:T(8,128)(2,1)S(1)}, bf16[128,128]{1,0:T(8,128)(2,1)S(1)}, u32[]{:S(2)}, u32[]{:S(2)}) collective-permute-start(bf16[128,128]{1,0:T(8,128)(2,1)S(1)} %shard_map.145), channel_id=1, source_target_pairs={{0,32},{32,64},{64,96},{96,128},{128,160},{160,192},{192,224},{224... | collective-permute-start | bytes 98312 | tf_op jit(solution)/shard_map/ppermute | solution.py:429
  118.2 5.9 %collective-permute-start.2 = (bf16[128,128]{1,0:T(8,128)(2,1)S(1)}, bf16[128,128]{1,0:T(8,128)(2,1)S(1)}, u32[]{:S(2)}, u32[]{:S(2)}) collective-permute-start(bf16[128,128]{1,0:T(8,128)(2,1)S(1)} %shard_map.149), channel_id=1, source_target_pairs={{0,32},{32,64},{64,96},{96,128},{128,160},{160,192},{192,224},{224... | collective-permute-start | bytes 98312 | tf_op jit(solution)/shard_map/ppermute | solution.py:429

commit v7 on v6

--- a/solution.py
+++ b/solution.py
@@ -25,12 +25,11 @@
 PEERS = ("core", "x", "tp")
 F32 = jnp.float32
 BF16 = jnp.bfloat16
-HIGH = lax.Precision.HIGHEST
-
-
-def dot(left, right, dims, precision=None):
+
+
+def dot(left, right, dims):
     return lax.dot_general(
-        left, right, ((dims[:1], dims[1:]), ((), ())), precision=precision, preferred_element_type=F32
+        left, right, ((dims[:1], dims[1:]), ((), ())), preferred_element_type=F32
     )
 
 
@@ -164,7 +163,8 @@
     decay = consts_ref[1:2, 3 * HEAD :]
     row = lax.broadcasted_iota(jnp.int32, (TOK, HEAD), 0).astype(F32)
     tail = turn_ref[0].astype(F32) * jnp.exp(-decay * (TOK - 1.0 - row))
-    update = dot(tail, turn_ref[1].astype(F32), (0, 0), HIGH) * HEAD**-0.5
+    queries = jnp.concatenate([turn_ref[1]] * 3, axis=0)
+    update = dot(pieces(tail, 3, 0), queries, (0, 0)) * HEAD**-0.5
     out_ref[...] = memory_ref[...] * jnp.exp(-decay * TOK) + update
 
 
@@ -199,8 +199,7 @@
     weights = jnp.where(causal, own_scores * jnp.exp(-decay * age), 0.0).astype(BF16)
     row = row.astype(F32)
     memory = memory_ref[...]
-    wide = queries.astype(F32)
-    raw = dot(weights, queries, (1, 0)) + dot(wide, memory, (1, 0), HIGH) * jnp.exp(
+    raw = dot(weights, queries, (1, 0)) + dot(jnp.concatenate([queries] * 3, axis=1), pieces(memory, 3, 0), (1, 0)) * jnp.exp(
         -decay * (row + 1.0)
     )
     spread = jnp.mean(raw * raw, axis=1, keepdims=True)

time: 125 us -> 125 us (level)
  no operation moved by 1% of the time
where the time goes in v7:
time: 125 us
  blocking collectives  79.2 us (63%)
  starting transfers between devices  17 us (14%)
  waiting for transfers between devices  14.2 us (11%)
  Pallas kernels  11.7 us (9%)
  between operations  1.39 us (1%)
    all_to_all x6, blocking collectives, exchanged(): return lax.all_to_all(value, axes, 0, 0, tiled=True)  79.2 us
    pallas_call x11, Pallas kernels, local_call(): pl.pallas_call(kernel, out_shape=outs, in_specs=[pl.BlockSpec(memory_spac...  11.7 us
    all_to_all x1, starting transfers between devices, exchanged(): return lax.all_to_all(value, axes, 0, 0, tiled=True)  10.8 us
    ppermute x2, waiting for transfers between devices, per_device(): passed = lax.ppermute(finished, 'section', onward)  10.5 us
    ppermute x2, starting transfers between devices, per_device(): passed = lax.ppermute(finished, 'section', onward)  3.84 us
    all_to_all x1, waiting for transfers between devices, exchanged(): return lax.all_to_all(value, axes, 0, 0, tiled=True)  3.74 us
  transfers between devices with their start and end apart: 4, of which 3 were waited for; matrix products, arithmetic and copies ran while one was open for 0% of the time, Pallas kernels for 3%

profile of v7, /device:TPU:1, one launch (start us, length us, event | category | flops | bytes accessed | tf_op | source)
XLA Modules:
  0.0 124.7 jit_solution(2598331878333096509)
XLA Ops:
  0.6 1.7 %shard_map.141 = bf16[8,144,128]{2,1,0:T(8,128)(2,1)} custom-call(bf16[128,128]{1,0:T(8,128)(2,1)} %bitcast.28, bf16[64,8,128]{2,1,0:T(8,128)(2,1)} %bitcast.26, bf16[64,8,128]{2,1,0:T(8,128)(2,1)} %bitcast.27), custom_call_target="tpu_custom_call" | custom-call | tf_op jit(solution)/shard_map/pallas_call | solution.py:306
  2.4 10.8 %all-to-all-start = ((bf16[8,144,128]{2,1,0:T(8,128)(2,1)}), bf16[8,144,128]{2,1,0:T(8,128)(2,1)}, u32[]{:S(2)}, u32[]{:S(2)}) async-start(bf16[8,144,128]{2,1,0:T(8,128)(2,1)} %shard_map.141), calls=%async_computation | async-start | bytes 589824 | tf_op jit(solution)/shard_map/all_to_all | solution.py:322
  13.9 2.0 %shard_map.140 = (bf16[432,4096]{1,0:T(8,128)(2,1)S(1)}, f32[8,128]{1,0:T(8,128)S(1)}) custom-call(f32[1,1]{1,0:T(1,128)S(6)} %copy.18.decay_ref, bf16[144,2,4096]{2,1,0:T(2,128)(2,1)} %bitcast.24, bf16[144,4096]{1,0:T(8,128)(2,1)} %bitcast.25), custom_call_target="tpu_custom_call" | custom-call | bytes 8388608 | tf_op jit(solution)/shard_map/pallas_call | solution.py:306
  15.9 0.6 copy-done.2
  16.5 3.7 %all-to-all-done.swapped_hbm = bf16[8,144,128]{2,1,0:T(8,128)(2,1)} async-done(((bf16[8,144,128]{2,1,0:T(8,128)(2,1)}), bf16[8,144,128]{2,1,0:T(8,128)(2,1)}, u32[]{:S(2)}, u32[]{:S(2)}) %all-to-all-start) | async-done | bytes 294944 | tf_op jit(solution)/shard_map/all_to_all | solution.py:322
  20.3 1.2 shard_map.142
  21.4 2.3 %collective-permute-start = (bf16[432,4096]{1,0:T(8,128)(2,1)S(1)}, bf16[432,4096]{1,0:T(8,128)(2,1)S(1)}, u32[]{:S(2)}, u32[]{:S(2)}) collective-permute-start(bf16[432,4096]{1,0:T(8,128)(2,1)S(1)} %get-tuple-element.29.near_ref), channel_id=1, source_target_pairs={{0,4},{4,0},{1,5},{5,1},{2,6},{6,2},{3,7},{7,3},{8,12},{12,8},{9,1... | collective-permute-start | bytes 10616840 | tf_op jit(solution)/shard_map/ppermute | solution.py:318
  23.7 6.6 %all_to_all.41 = f32[4,8,128]{2,1,0:T(8,128)S(1)} all-to-all(f32[4,8,128]{2,1,0:T(8,128)S(1)} %get-tuple-element.23), channel_id=1, replica_groups=mesh['section'=16,'x'=4,'core'=2,'tp'=4] {'tp'}, dimensions={0} | all-to-all | bytes 32768 | tf_op jit(solution)/shard_map/all_to_all | solution.py:322
  30.3 0.9 shard_map.143
  31.2 16.0 %all_to_all.42.rows_ref = bf16[32,64,128]{2,1,0:T(8,128)(2,1)S(1)} all-to-all(bf16[32,64,128]{2,1,0:T(8,128)(2,1)S(1)} %get-tuple-element.28), channel_id=1, replica_groups=mesh['section'=16,'x'=4,'core'=2,'tp'=4] {'core','x','tp'}, dimensions={0} | all-to-all | bytes 1048576 | tf_op jit(solution)/shard_map/all_to_all | solution.py:322
  47.1 1.9 %shard_map.144 = bf16[32,64,128]{2,1,0:T(8,128)(2,1)S(1)} custom-call(bf16[32,64,128]{2,1,0:T(8,128)(2,1)S(1)} %all_to_all.42.rows_ref, f32[1,4096]{1,0:T(1,128)S(1)} %copy-done, bf16[432,4096]{1,0:T(8,128)(2,1)S(1)} %get-tuple-element.29.near_ref, bf16[432,4096]{1,0:T(8,128)(2,1)S(1)} %collective-permute-done.far_ref), custom_call_target="tpu_custom_call" | custom-call | tf_op jit(solution)/shard_map/pallas_call | solution.py:306
  49.1 15.1 %all_to_all.43.parts_ref = bf16[32,64,128]{2,1,0:T(8,128)(2,1)S(1)} all-to-all(bf16[32,64,128]{2,1,0:T(8,128)(2,1)S(1)} %shard_map.144), channel_id=1, replica_groups=mesh['section'=16,'x'=4,'core'=2,'tp'=4] {'core','x','tp'}, dimensions={0} | all-to-all | bytes 1048576 | tf_op jit(solution)/shard_map/all_to_all | solution.py:322
  64.2 1.9 %collective-permute-start.1 = (bf16[128,128]{1,0:T(8,128)(2,1)S(1)}, bf16[128,128]{1,0:T(8,128)(2,1)S(1)}, u32[]{:S(2)}, u32[]{:S(2)}) collective-permute-start(bf16[128,128]{1,0:T(8,128)(2,1)S(1)} %shard_map.145), channel_id=1, source_target_pairs={{0,32},{32,64},{64,96},{96,128},{128,160},{160,192},{192,224},{224... | collective-permute-start | bytes 98312 | tf_op jit(solution)/shard_map/ppermute | solution.py:428
  66.2 7.4 %collective-permute-done.1.passed_ref = bf16[128,128]{1,0:T(8,128)(2,1)S(1)} collective-permute-done((bf16[128,128]{1,0:T(8,128)(2,1)S(1)}, bf16[128,128]{1,0:T(8,128)(2,1)S(1)}, u32[]{:S(2)}, u32[]{:S(2)}) %collective-permute-start.1) | collective-permute-done | bytes 32800 | tf_op jit(solution)/shard_map/ppermute | solution.py:428
  73.6 0.1 shard_map.146
  73.7 11.6 %all_to_all.44 = f32[32,1,128]{2,1,0:T(1,128)S(1)} all-to-all(f32[32,1,128]{2,1,0:T(1,128)S(1)} %bitcast.23), channel_id=1, replica_groups=mesh['section'=16,'x'=4,'core'=2,'tp'=4] {'core','x','tp'}, dimensions={0} | all-to-all | bytes 32768 | tf_op jit(solution)/shard_map/all_to_all | solution.py:322
  85.3 0.8 shard_map.147
  86.2 14.9 %all_to_all.45.rows_ref = bf16[32,64,128]{2,1,0:T(8,128)(2,1)S(1)} all-to-all(bf16[32,64,128]{2,1,0:T(8,128)(2,1)S(1)} %get-tuple-element.35), channel_id=1, replica_groups=mesh['section'=16,'x'=4,'core'=2,'tp'=4] {'core','x','tp'}, dimensions={0} | all-to-all | bytes 1048576 | tf_op jit(solution)/shard_map/all_to_all | solution.py:322
  101.1 1.9 %shard_map.148 = bf16[32,64,128]{2,1,0:T(8,128)(2,1)S(1)} custom-call(bf16[32,64,128]{2,1,0:T(8,128)(2,1)S(1)} %all_to_all.45.rows_ref, f32[1,4096]{1,0:T(1,128)S(1)} %copy-done, bf16[432,4096]{1,0:T(8,128)(2,1)S(1)} %get-tuple-element.29.near_ref, bf16[432,4096]{1,0:T(8,128)(2,1)S(1)} %collective-permute-done.far_ref), custom_call_target="tpu_custom_call" | custom-call | tf_op jit(solution)/shard_map/pallas_call | solution.py:306
  103.0 15.1 %all_to_all.46.parts_ref = bf16[32,64,128]{2,1,0:T(8,128)(2,1)S(1)} all-to-all(bf16[32,64,128]{2,1,0:T(8,128)(2,1)S(1)} %shard_map.148), channel_id=1, replica_groups=mesh['section'=16,'x'=4,'core'=2,'tp'=4] {'core','x','tp'}, dimensions={0} | all-to-all | bytes 1048576 | tf_op jit(solution)/shard_map/all_to_all | solution.py:322
  118.2 1.9 %collective-permute-start.2 = (bf16[128,128]{1,0:T(8,128)(2,1)S(1)}, bf16[128,128]{1,0:T(8,128)(2,1)S(1)}, u32[]{:S(2)}, u32[]{:S(2)}) collective-permute-start(bf16[128,128]{1,0:T(8,128)(2,1)S(1)} %shard_map.149), channel_id=1, source_target_pairs={{0,32},{32,64},{64,96},{96,128},{128,160},{160,192},{192,224},{224... | collective-permute-start | bytes 98312 | tf_op jit(solution)/shard_map/ppermute | solution.py:428
  120.1 0.9 shard_map.150
  121.0 3.1 %collective-permute-done.2 = bf16[128,128]{1,0:T(8,128)(2,1)S(1)} collective-permute-done((bf16[128,128]{1,0:T(8,128)(2,1)S(1)}, bf16[128,128]{1,0:T(8,128)(2,1)S(1)}, u32[]{:S(2)}, u32[]{:S(2)}) %collective-permute-start.2) | collective-permute-done | bytes 32800 | tf_op jit(solution)/shard_map/ppermute | solution.py:428
  124.1 0.6 maximum_bitcast_fusion
  (8 shorter events, 0.2 us)
Async XLA Ops:
  0.6 46.5 %copy-start = (f32[1,4096]{1,0:T(1,128)S(1)}, f32[1,4096]{1,0:T(1,128)}, u32[]{:S(2)}) copy-start(f32[1,4096]{1,0:T(1,128)} %gain_ref.3) | copy-start | bytes 49156
  2.4 17.9 %all-to-all-start = ((bf16[8,144,128]{2,1,0:T(8,128)(2,1)}), bf16[8,144,128]{2,1,0:T(8,128)(2,1)}, u32[]{:S(2)}, u32[]{:S(2)}) async-start(bf16[8,144,128]{2,1,0:T(8,128)(2,1)} %shard_map.141), calls=%async_computation | async-start | bytes 589824 | tf_op jit(solution)/shard_map/all_to_all | solution.py:322
  15.9 0.6 copy-start.2
  21.4 25.7 %collective-permute-start = (bf16[432,4096]{1,0:T(8,128)(2,1)S(1)}, bf16[432,4096]{1,0:T(8,128)(2,1)S(1)}, u32[]{:S(2)}, u32[]{:S(2)}) collective-permute-start(bf16[432,4096]{1,0:T(8,128)(2,1)S(1)} %get-tuple-element.29.near_ref), channel_id=1, source_target_pairs={{0,4},{4,0},{1,5},{5,1},{2,6},{6,2},{3,7},{7,3},{8,12},{12,8},{9,1... | collective-permute-start | bytes 10616840 | tf_op jit(solution)/shard_map/ppermute | solution.py:318
  47.1 26.4 %copy-start.1 = (bf16[1,128,128]{2,1,0:T(8,128)(2,1)S(1)}, bf16[1,128,128]{2,1,0:T(8,128)(2,1)}, u32[]{:S(2)}) copy-start(bf16[1,128,128]{2,1,0:T(8,128)(2,1)} %param.14) | copy-start | bytes 98308
  64.2 9.3 %collective-permute-start.1 = (bf16[128,128]{1,0:T(8,128)(2,1)S(1)}, bf16[128,128]{1,0:T(8,128)(2,1)S(1)}, u32[]{:S(2)}, u32[]{:S(2)}) collective-permute-start(bf16[128,128]{1,0:T(8,128)(2,1)S(1)} %shard_map.145), channel_id=1, source_target_pairs={{0,32},{32,64},{64,96},{96,128},{128,160},{160,192},{192,224},{224... | collective-permute-start | bytes 98312 | tf_op jit(solution)/shard_map/ppermute | solution.py:428
  118.2 5.9 %collective-permute-start.2 = (bf16[128,128]{1,0:T(8,128)(2,1)S(1)}, bf16[128,128]{1,0:T(8,128)(2,1)S(1)}, u32[]{:S(2)}, u32[]{:S(2)}) collective-permute-start(bf16[128,128]{1,0:T(8,128)(2,1)S(1)} %shard_map.149), channel_id=1, source_target_pairs={{0,32},{32,64},{64,96},{96,128},{128,160},{160,192},{192,224},{224... | collective-permute-start | bytes 98312 | tf_op jit(solution)/shard_map/ppermute | solution.py:428
